TPU v7x, 256 devices: a whole 4x4x8 slice. The times are simulated.
256 devices in a mesh: space: 32 (over y, z_hi, core), slab: 8 (over x, z_lo).
Axes of the slice: x: 4, y: 4, z: 8 (z_hi: 4, z_lo: 2; z = z_hi * 2 + z_lo), core: 2. Of those that a mesh axis runs over, the one named last changes fastest.
Arguments:
- latents: bfloat16 [131072, 512], P(('space', 'slab')), may hold values from -6 to 6
- upstream: bfloat16 [131072, 512], P(('space', 'slab')), may hold values from -6 to 6
- msg_weight: bfloat16 [2, 512, 512], replicated, may hold values from -0.25 to 0.25
- self_weight: bfloat16 [2, 512, 512], replicated, may hold values from -0.25 to 0.25
- agg_weight: bfloat16 [2, 512, 512], replicated, may hold values from -0.25 to 0.25
- out_weight: bfloat16 [2, 512, 512], replicated, may hold values from -0.25 to 0.25
- gains: float32 [2, 512], replicated, may hold values from 0.25 to 1.75
- edge_weight: bfloat16 [1024, 6, 128, 128], P(('space', 'slab')), as said below
- nbr_slot: int32 [1024, 6], P(('space', 'slab')), may hold values from 0 to 11, as said below
- send_list: int32 [32, 8, 4, 2], P('space', 'slab'), may hold values from 0 to 3, as said below
Outputs:
- latents_out: bfloat16 [131072, 512], P(('space', 'slab'))
- latent_grad: float32 [131072, 512], P(('space', 'slab'))
- grad_msg: float32 [2, 512, 512], P(None, 'space')
- grad_self: float32 [2, 512, 512], P(None, 'space')
- grad_agg: float32 [2, 512, 512], P(None, 'space')
- grad_out: float32 [2, 512, 512], P(None, 'space')
- grad_gain: float32 [2, 512], P(None, 'space')
Inputs may be any that keep to these rules, and one draw needn't show every extreme that they name: `nbr_slot`: entry [b, k] indexes the extended list of block b's device: 0 to 3 its own blocks, then 2 entries each from the lower and upper space neighbour and the lower and upper slab neighbour, in that order; entries of a missing neighbour are never named. `send_list`: entry [s, l, d, t] is a local block index that device (s, l) sends: d = 0 to space index s + 1, d = 1 to s - 1, d = 2 to slab index l + 1, d = 3 to l - 1; the 2 entries of one row are distinct. `edge_weight`: tile [b, k] has the rows of block b as first index and the rows of the source block as second index.
All inputs are finite; a program needn't handle non-finite values.
Results may differ from a plain program's by a relative error of at most 0.039.
Values may be sent and summed in bfloat16 or wider, within the bound.
A program may use at most 128 MiB of HBM per device.

v0:
```python
import jax
import jax.numpy as jnp
from jax import lax
from jax.sharding import PartitionSpec as P

EPS = 1e-05


def shifted(block, axis, distance):
    devices = range(lax.axis_size(axis))
    route = [(i - distance, i) for i in devices if i - distance in devices]
    return lax.ppermute(block, axis, route)


def silu_slope(value):
    sigma = jax.nn.sigmoid(value)
    return sigma * (1.0 + value * (1.0 - sigma))


def layer_norm(update):
    mean_value = jnp.mean(update, axis=-1, keepdims=True)
    centred = update - mean_value
    inverse = lax.rsqrt(jnp.mean(centred * centred, axis=-1, keepdims=True) + EPS)
    return (centred * inverse, inverse)


def forward_layer(latent, weights, edge_weight, nbr_slot, sends):
    msg_w, self_w, agg_w, out_w, gain_row = weights
    block_count = edge_weight.shape[0]
    tile_count = edge_weight.shape[1]
    block_rows = edge_weight.shape[2]
    feature_count = latent.shape[1]
    pre_msg = jnp.dot(latent, msg_w, preferred_element_type=jnp.float32)
    message = (
        jax.nn.silu(pre_msg).astype(jnp.bfloat16).reshape(block_count, block_rows, feature_count)
    )
    lower_space = shifted(jnp.take(message, sends[0], axis=0), "space", 1)
    upper_space = shifted(jnp.take(message, sends[1], axis=0), "space", -1)
    lower_slab = shifted(jnp.take(message, sends[2], axis=0), "slab", 1)
    upper_slab = shifted(jnp.take(message, sends[3], axis=0), "slab", -1)
    extended = jnp.concatenate([message, lower_space, upper_space, lower_slab, upper_slab], axis=0)
    source = jnp.take(extended, nbr_slot.reshape(-1), axis=0).reshape(
        block_count, tile_count, block_rows, feature_count
    )
    merged_sum = jnp.einsum(
        "bkij,bkjw->biw", edge_weight, source, preferred_element_type=jnp.float32
    )
    merged = merged_sum.reshape(block_count * block_rows, feature_count).astype(jnp.bfloat16)
    pre_hidden = jnp.dot(latent, self_w, preferred_element_type=jnp.float32) + jnp.dot(
        merged, agg_w, preferred_element_type=jnp.float32
    )
    hidden = jax.nn.silu(pre_hidden).astype(jnp.bfloat16)
    update = jnp.dot(hidden, out_w, preferred_element_type=jnp.float32)
    normed, inverse = layer_norm(update)
    output = (latent.astype(jnp.float32) + gain_row * normed).astype(jnp.bfloat16)
    return (output, (latent, pre_msg, merged, pre_hidden, hidden, normed, inverse))


def backward_layer(grad_y, saved, weights, edge_weight, nbr_slot, sends):
    latent, pre_msg, merged, pre_hidden, hidden, normed, inverse = saved
    msg_w, self_w, agg_w, out_w, gain_row = weights
    block_count = edge_weight.shape[0]
    tile_count = edge_weight.shape[1]
    block_rows = edge_weight.shape[2]
    feature_count = latent.shape[1]
    halo_count = sends.shape[1]
    slot_count = block_count + 4 * halo_count
    grad_gain_row = jnp.sum(grad_y * normed, axis=0)
    grad_norm = grad_y * gain_row
    grad_update = inverse * (
        grad_norm
        - jnp.mean(grad_norm, axis=-1, keepdims=True)
        - normed * jnp.mean(grad_norm * normed, axis=-1, keepdims=True)
    )
    grad_update = grad_update.astype(jnp.bfloat16)
    grad_out_w = jnp.dot(hidden.T, grad_update, preferred_element_type=jnp.float32)
    grad_pre_hidden = jnp.dot(
        grad_update, out_w.T, preferred_element_type=jnp.float32
    ) * silu_slope(pre_hidden)
    grad_pre_hidden = grad_pre_hidden.astype(jnp.bfloat16)
    grad_self_w = jnp.dot(latent.T, grad_pre_hidden, preferred_element_type=jnp.float32)
    grad_agg_w = jnp.dot(merged.T, grad_pre_hidden, preferred_element_type=jnp.float32)
    grad_merged = jnp.dot(grad_pre_hidden, agg_w.T, preferred_element_type=jnp.float32).astype(
        jnp.bfloat16
    )
    grad_merged = grad_merged.reshape(block_count, block_rows, feature_count)
    contrib = jnp.einsum(
        "bkij,biw->bkjw", edge_weight, grad_merged, preferred_element_type=jnp.float32
    )
    contrib = contrib.reshape(block_count * tile_count, block_rows, feature_count)
    slot_range = jnp.arange(slot_count, dtype=jnp.int32)
    chooser = (nbr_slot.reshape(-1)[:, None] == slot_range[None, :]).astype(jnp.float32)
    grad_extended = jnp.einsum("ce,cjw->ejw", chooser, contrib, precision=lax.Precision.HIGHEST)
    halo_grad = (
        grad_extended[block_count:]
        .astype(jnp.bfloat16)
        .reshape(4, halo_count, block_rows, feature_count)
    )
    back_lower_space = shifted(halo_grad[0], "space", -1)
    back_upper_space = shifted(halo_grad[1], "space", 1)
    back_lower_slab = shifted(halo_grad[2], "slab", -1)
    back_upper_slab = shifted(halo_grad[3], "slab", 1)
    returned = [back_lower_space, back_upper_space, back_lower_slab, back_upper_slab]
    block_range = jnp.arange(block_count, dtype=jnp.int32)
    grad_message = grad_extended[:block_count]
    for direction in range(4):
        picker = (sends[direction][:, None] == block_range[None, :]).astype(jnp.float32)
        grad_message = grad_message + jnp.einsum(
            "tb,tjw->bjw",
            picker,
            returned[direction].astype(jnp.float32),
            precision=lax.Precision.HIGHEST,
        )
    grad_pre_msg = (
        grad_message.reshape(block_count * block_rows, feature_count) * silu_slope(pre_msg)
    ).astype(jnp.bfloat16)
    grad_msg_w = jnp.dot(latent.T, grad_pre_msg, preferred_element_type=jnp.float32)
    grad_x = (
        grad_y
        + jnp.dot(grad_pre_hidden, self_w.T, preferred_element_type=jnp.float32)
        + jnp.dot(grad_pre_msg, msg_w.T, preferred_element_type=jnp.float32)
    )
    return (grad_x, (grad_msg_w, grad_self_w, grad_agg_w, grad_out_w, grad_gain_row))


def reduce_grads(parts):
    shares = (
        lax.psum_scatter(
            parts[0].astype(jnp.bfloat16), "space", scatter_dimension=0, tiled=True
        ).astype(jnp.float32),
        lax.psum_scatter(
            parts[1].astype(jnp.bfloat16), "space", scatter_dimension=0, tiled=True
        ).astype(jnp.float32),
        lax.psum_scatter(
            parts[2].astype(jnp.bfloat16), "space", scatter_dimension=0, tiled=True
        ).astype(jnp.float32),
        lax.psum_scatter(
            parts[3].astype(jnp.bfloat16), "space", scatter_dimension=0, tiled=True
        ).astype(jnp.float32),
        lax.psum_scatter(
            parts[4].astype(jnp.bfloat16), "space", scatter_dimension=0, tiled=True
        ).astype(jnp.float32),
    )
    summed = (
        lax.psum(shares[0].astype(jnp.bfloat16), "slab").astype(jnp.float32),
        lax.psum(shares[1].astype(jnp.bfloat16), "slab").astype(jnp.float32),
        lax.psum(shares[2].astype(jnp.bfloat16), "slab").astype(jnp.float32),
        lax.psum(shares[3].astype(jnp.bfloat16), "slab").astype(jnp.float32),
        lax.psum(shares[4].astype(jnp.bfloat16), "slab").astype(jnp.float32),
    )
    return (summed[0], summed[1], summed[2], summed[3], summed[4])


def local(
    latents,
    upstream,
    msg_weight,
    self_weight,
    agg_weight,
    out_weight,
    gains,
    edge_weight,
    nbr_slot,
    send_list,
):
    sends = send_list.reshape(4, send_list.shape[-1])
    layer_count = msg_weight.shape[0]
    latent = latents
    saved_all = []
    for layer in range(layer_count):
        weights = (
            msg_weight[layer],
            self_weight[layer],
            agg_weight[layer],
            out_weight[layer],
            gains[layer],
        )
        latent, saved = forward_layer(latent, weights, edge_weight, nbr_slot, sends)
        saved_all.append(saved)
    grad_now = upstream.astype(jnp.float32)
    collected = [None] * layer_count
    for layer in reversed(range(layer_count)):
        weights = (
            msg_weight[layer],
            self_weight[layer],
            agg_weight[layer],
            out_weight[layer],
            gains[layer],
        )
        grad_now, parts = backward_layer(
            grad_now, saved_all[layer], weights, edge_weight, nbr_slot, sends
        )
        collected[layer] = parts
    collected = [reduce_grads(parts) for parts in collected]
    stacks = [jnp.stack([parts[index] for parts in collected]) for index in range(5)]
    return (latent, grad_now, stacks[0], stacks[1], stacks[2], stacks[3], stacks[4])


def solution(mesh):
    return jax.shard_map(
        local,
        mesh=mesh,
        in_specs=(
            P(("space", "slab"), None),
            P(("space", "slab"), None),
            P(),
            P(),
            P(),
            P(),
            P(),
            P(("space", "slab"), None, None, None),
            P(("space", "slab"), None),
            P("space", "slab", None, None),
        ),
        out_specs=(
            P(("space", "slab"), None),
            P(("space", "slab"), None),
            P(None, "space", None),
            P(None, "space", None),
            P(None, "space", None),
            P(None, "space", None),
            P(None, "space"),
        ),
        check_vma=False,
    )
```

profile of v0, /device:TPU:8, one launch (start us, length us, event | category | flops | bytes accessed | tf_op | source)
XLA Modules:
  0.0 947.4 jit_solution(10392987223712579921)
XLA Ops:
  15.7 7.5 collective-permute-start.1
  38.1 4.2 collective-permute-done.3
  64.7 6.7 collective-permute-start.5
  79.8 9.7 %collective-permute-done.7 = bf16[2,128,512]{2,1,0:T(8,128)(2,1)S(1)} collective-permute-done((bf16[2,128,512]{2,1,0:T(8,128)(2,1)S(1)}, bf16[2,128,512]{2,1,0:T(8,128)(2,1)S(1)}, u32[]{:S(2)}, u32[]{:S(2)}) %collective-permute-start.7) | collective-permute-done | bytes 262176 | tf_op jit(solution)/shard_map/ppermute | solution.py:12
  90.3 3.9 gather_fusion.9
  103.9 3.6 fusion.96
  107.5 6.7 copy.36
  114.2 7.4 fusion.94
  128.0 6.7 collective-permute-start.8
  134.6 4.8 collective-permute-start.11
  152.7 3.7 fusion.97
  156.3 6.8 copy.40
  164.4 7.5 fusion.95
  178.4 6.6 collective-permute-start.12
  185.1 7.1 collective-permute-start.15
  215.1 60.2 %all-reduce.2 = (bf16[512]{0:T(512)(128)(2,1)S(1)}, bf16[512]{0:T(512)(128)(2,1)S(1)}) all-reduce(bf16[512]{0:T(512)(128)(2,1)S(1)} %get-tuple-element.25, bf16[512]{0:T(512)(128)(2,1)S(1)} %get-tuple-element.23), channel_id=11, replica_groups=mesh['space'=32,'slab'=8] {'space'}, use_global_device_ids=true, to_apply=%region_28.31.clone | all-reduce | flops 1024 | bytes 4096
  279.5 29.1 %reduce-scatter.27.cloned.1.call-done = bf16[16,512]{1,0:T(8,128)(2,1)} async-done(((bf16[512,512]{1,0:T(8,128)(2,1)}), bf16[16,512]{1,0:T(8,128)(2,1)}) %reduce-scatter.27.cloned.1.call-update) | async-done | bytes 16400
  310.1 88.2 %reduce-scatter.29.cloned.1.call-done = bf16[16,512]{1,0:T(8,128)(2,1)} async-done(((bf16[512,512]{1,0:T(8,128)(2,1)}), bf16[16,512]{1,0:T(8,128)(2,1)}) %reduce-scatter.29.cloned.1.call-update) | async-done | bytes 16400
  399.7 88.0 %reduce-scatter.25.cloned.1.call-done = bf16[16,512]{1,0:T(8,128)(2,1)} async-done(((bf16[512,512]{1,0:T(8,128)(2,1)}), bf16[16,512]{1,0:T(8,128)(2,1)}) %reduce-scatter.25.cloned.1.call-update) | async-done | bytes 16400
  489.2 87.9 %reduce-scatter.19.cloned.1.call-done = bf16[16,512]{1,0:T(8,128)(2,1)} async-done(((bf16[512,512]{1,0:T(8,128)(2,1)}), bf16[16,512]{1,0:T(8,128)(2,1)}) %reduce-scatter.19.cloned.1.call-update) | async-done | bytes 16400 | tf_op jit(solution)/shard_map/reduce_scatter | solution.py:134
  577.2 89.4 %reduce-scatter.23.cloned.1.call-done = bf16[16,512]{1,0:T(8,128)(2,1)} async-done(((bf16[512,512]{1,0:T(8,128)(2,1)}), bf16[16,512]{1,0:T(8,128)(2,1)}) %reduce-scatter.23.cloned.1.call-update) | async-done | bytes 16400 | tf_op jit(solution)/shard_map/reduce_scatter | solution.py:137
  666.6 89.6 %reduce-scatter.17.cloned.1.call-done = bf16[16,512]{1,0:T(8,128)(2,1)} async-done(((bf16[512,512]{1,0:T(8,128)(2,1)}), bf16[16,512]{1,0:T(8,128)(2,1)}) %reduce-scatter.17.cloned.1.call-update) | async-done | bytes 16400 | tf_op jit(solution)/shard_map/reduce_scatter | solution.py:134
  756.2 89.6 %reduce-scatter.21.cloned.1.call-done = bf16[16,512]{1,0:T(8,128)(2,1)} async-done(((bf16[512,512]{1,0:T(8,128)(2,1)}), bf16[16,512]{1,0:T(8,128)(2,1)}) %reduce-scatter.21.cloned.1.call-update) | async-done | bytes 16400 | tf_op jit(solution)/shard_map/reduce_scatter | solution.py:137
  848.9 82.8 %all-reduce.6.cloned.1.call-done = (bf16[1,16,512]{1,2,0:T(8,128)(2,1)}, bf16[1,16,512]{1,2,0:T(8,128)(2,1)}, bf16[1,16,512]{1,2,0:T(8,128)(2,1)}, bf16[1,16,512...) async-done(((bf16[1,16,512]{1,2,0:T(8,128)(2,1)}, ...) | async-done | bytes 131152 | tf_op jit(solution)/shard_map/psum | solution.py:145
  (248 shorter events, 134.1 us)
Async XLA Ops:
  7.2 270.8 %reduce-scatter.31.cloned.1.call-start = ((), (), s32[]{:S(2)}) async-start(), calls=%async_computation.15 | async-start | bytes 540672
  12.4 22.7 %collective-permute-start = (bf16[2,128,512]{2,1,0:T(8,128)(2,1)}, bf16[2,128,512]{2,1,0:T(8,128)(2,1)}, u32[]{:S(2)}, u32[]{:S(2)}) collective-permute-start(bf16[2,128,512]{2,1,0:T(8,128)(2,1)} %broadcast_select_fusion.9), channel_id=1, source_target_pairs={{0,8},{8,16},{16,24},{24,32},{32,40},{40,48},{48,56},{56,64},{64,7... | collective-permute-start | bytes 786440 | tf_op jit(solution)/shard_map/ppermute | solution.py:12
  15.7 20.4 %collective-permute-start.1 = (bf16[2,128,512]{2,1,0:T(8,128)(2,1)}, bf16[2,128,512]{2,1,0:T(8,128)(2,1)}, u32[]{:S(2)}, u32[]{:S(2)}) collective-permute-start(bf16[2,128,512]{2,1,0:T(8,128)(2,1)} %broadcast_select_fusion.7), channel_id=1, source_target_pairs={{8,0},{16,8},{24,16},{32,24},{40,32},{48,40},{56,48},{64,56},{72,6... | collective-permute-start | bytes 786440 | tf_op jit(solution)/shard_map/ppermute | solution.py:12
  24.7 12.4 %collective-permute-start.2 = (bf16[2,128,512]{2,1,0:T(8,128)(2,1)}, bf16[2,128,512]{2,1,0:T(8,128)(2,1)}, u32[]{:S(2)}, u32[]{:S(2)}) collective-permute-start(bf16[2,128,512]{2,1,0:T(8,128)(2,1)} %broadcast_select_fusion.5), channel_id=1, source_target_pairs={{0,1},{1,2},{2,3},{3,4},{4,5},{5,6},{6,7},{8,9},{9,10},{10,11},{11... | collective-permute-start | bytes 786440 | tf_op jit(solution)/shard_map/ppermute | solution.py:12
  29.7 12.6 %collective-permute-start.3 = (bf16[2,128,512]{2,1,0:T(8,128)(2,1)}, bf16[2,128,512]{2,1,0:T(8,128)(2,1)}, u32[]{:S(2)}, u32[]{:S(2)}) collective-permute-start(bf16[2,128,512]{2,1,0:T(8,128)(2,1)} %broadcast_select_fusion.3), channel_id=1, source_target_pairs={{1,0},{2,1},{3,2},{4,3},{5,4},{6,5},{7,6},{9,8},{10,9},{11,10},{12... | collective-permute-start | bytes 786440 | tf_op jit(solution)/shard_map/ppermute | solution.py:12
  62.8 13.4 %collective-permute-start.4 = (bf16[2,128,512]{2,1,0:T(8,128)(2,1)S(1)}, bf16[2,128,512]{2,1,0:T(8,128)(2,1)S(1)}, u32[]{:S(2)}, u32[]{:S(2)}) collective-permute-start(bf16[2,128,512]{2,1,0:T(8,128)(2,1)S(1)} %broadcast_select_fusion.8), channel_id=1, source_target_pairs={{0,8},{8,16},{16,24},{24,32},{32,40},{40,48},{48,56},{56,64},{64,7... | collective-permute-start | bytes 786440 | tf_op jit(solution)/shard_map/ppermute | solution.py:12
  64.7 12.4 %collective-permute-start.5 = (bf16[2,128,512]{2,1,0:T(8,128)(2,1)S(1)}, bf16[2,128,512]{2,1,0:T(8,128)(2,1)S(1)}, u32[]{:S(2)}, u32[]{:S(2)}) collective-permute-start(bf16[2,128,512]{2,1,0:T(8,128)(2,1)S(1)} %broadcast_select_fusion.6), channel_id=1, source_target_pairs={{8,0},{16,8},{24,16},{32,24},{40,32},{48,40},{56,48},{64,56},{72,6... | collective-permute-start | bytes 786440 | tf_op jit(solution)/shard_map/ppermute | solution.py:12
  74.7 14.8 %collective-permute-start.7 = (bf16[2,128,512]{2,1,0:T(8,128)(2,1)S(1)}, bf16[2,128,512]{2,1,0:T(8,128)(2,1)S(1)}, u32[]{:S(2)}, u32[]{:S(2)}) collective-permute-start(bf16[2,128,512]{2,1,0:T(8,128)(2,1)S(1)} %broadcast_select_fusion.2), channel_id=1, source_target_pairs={{1,0},{2,1},{3,2},{4,3},{5,4},{6,5},{7,6},{9,8},{10,9},{11,10},{12... | collective-permute-start | bytes 786440 | tf_op jit(solution)/shard_map/ppermute | solution.py:12
  123.4 16.6 %collective-permute-start.10 = (bf16[2,128,512]{2,0,1:T(2,128)(2,1)}, bf16[2,128,512]{2,0,1:T(2,128)(2,1)S(1)}, u32[]{:S(2)}, u32[]{:S(2)}) collective-permute-start(bf16[2,128,512]{2,0,1:T(2,128)(2,1)} %get-tuple-element.51), channel_id=1, source_target_pairs={{1,0},{2,1},{3,2},{4,3},{5,4},{6,5},{7,6},{9,8},{10,9},{11,10},{12... | collective-permute-start | bytes 786440 | tf_op jit(solution)/shard_map/ppermute | solution.py:12
  124.7 14.7 %collective-permute-start.9 = (bf16[2,128,512]{2,0,1:T(2,128)(2,1)}, bf16[2,128,512]{2,0,1:T(2,128)(2,1)S(1)}, u32[]{:S(2)}, u32[]{:S(2)}) collective-permute-start(bf16[2,128,512]{2,0,1:T(2,128)(2,1)} %get-tuple-element.52), channel_id=1, source_target_pairs={{0,8},{8,16},{16,24},{24,32},{32,40},{40,48},{48,56},{56,64},{64,7... | collective-permute-start | bytes 786440 | tf_op jit(solution)/shard_map/ppermute | solution.py:12
  127.9 180.7 %reduce-scatter.27.cloned.1.call-start = ((), (), s32[]{:S(2)}) async-start(), calls=%async_computation.13 | async-start | bytes 540672
  128.0 16.7 %collective-permute-start.8 = (bf16[2,128,512]{2,0,1:T(2,128)(2,1)}, bf16[2,128,512]{2,0,1:T(2,128)(2,1)S(1)}, u32[]{:S(2)}, u32[]{:S(2)}) collective-permute-start(bf16[2,128,512]{2,0,1:T(2,128)(2,1)} %get-tuple-element.49), channel_id=1, source_target_pairs={{8,0},{16,8},{24,16},{32,24},{40,32},{48,40},{56,48},{64,56},{72,6... | collective-permute-start | bytes 786440 | tf_op jit(solution)/shard_map/ppermute | solution.py:12
  134.6 9.5 %collective-permute-start.11 = (bf16[2,128,512]{2,0,1:T(2,128)(2,1)}, bf16[2,128,512]{2,0,1:T(2,128)(2,1)S(1)}, u32[]{:S(2)}, u32[]{:S(2)}) collective-permute-start(bf16[2,128,512]{2,0,1:T(2,128)(2,1)} %get-tuple-element.50), channel_id=1, source_target_pairs={{0,1},{1,2},{2,3},{3,4},{4,5},{5,6},{6,7},{8,9},{9,10},{10,11},{11... | collective-permute-start | bytes 786440 | tf_op jit(solution)/shard_map/ppermute | solution.py:12
  164.4 233.9 %reduce-scatter.29.cloned.1.call-start = ((), (), s32[]{:S(2)}) async-start(), calls=%async_computation.14 | async-start | bytes 540672
  173.7 20.3 %collective-permute-start.14 = (bf16[2,128,512]{2,0,1:T(2,128)(2,1)}, bf16[2,128,512]{2,0,1:T(2,128)(2,1)}, u32[]{:S(2)}, u32[]{:S(2)}) collective-permute-start(bf16[2,128,512]{2,0,1:T(2,128)(2,1)} %get-tuple-element.47), channel_id=1, source_target_pairs={{1,0},{2,1},{3,2},{4,3},{5,4},{6,5},{7,6},{9,8},{10,9},{11,10},{12... | collective-permute-start | bytes 786440 | tf_op jit(solution)/shard_map/ppermute | solution.py:12
  175.0 17.5 %collective-permute-start.13 = (bf16[2,128,512]{2,0,1:T(2,128)(2,1)}, bf16[2,128,512]{2,0,1:T(2,128)(2,1)}, u32[]{:S(2)}, u32[]{:S(2)}) collective-permute-start(bf16[2,128,512]{2,0,1:T(2,128)(2,1)} %get-tuple-element.48), channel_id=1, source_target_pairs={{0,8},{8,16},{16,24},{24,32},{32,40},{40,48},{48,56},{56,64},{64,7... | collective-permute-start | bytes 786440 | tf_op jit(solution)/shard_map/ppermute | solution.py:12
  178.4 18.9 %collective-permute-start.12 = (bf16[2,128,512]{2,0,1:T(2,128)(2,1)}, bf16[2,128,512]{2,0,1:T(2,128)(2,1)S(1)}, u32[]{:S(2)}, u32[]{:S(2)}) collective-permute-start(bf16[2,128,512]{2,0,1:T(2,128)(2,1)} %get-tuple-element.45), channel_id=1, source_target_pairs={{8,0},{16,8},{24,16},{32,24},{40,32},{48,40},{56,48},{64,56},{72,6... | collective-permute-start | bytes 786440 | tf_op jit(solution)/shard_map/ppermute | solution.py:12
  185.1 11.7 %collective-permute-start.15 = (bf16[2,128,512]{2,0,1:T(2,128)(2,1)}, bf16[2,128,512]{2,0,1:T(2,128)(2,1)S(1)}, u32[]{:S(2)}, u32[]{:S(2)}) collective-permute-start(bf16[2,128,512]{2,0,1:T(2,128)(2,1)} %get-tuple-element.46), channel_id=1, source_target_pairs={{0,1},{1,2},{2,3},{3,4},{4,5},{5,6},{6,7},{8,9},{9,10},{10,11},{11... | collective-permute-start | bytes 786440 | tf_op jit(solution)/shard_map/ppermute | solution.py:12
  192.2 295.6 %reduce-scatter.25.cloned.1.call-start = ((), (), s32[]{:S(2)}) async-start(), calls=%async_computation.12 | async-start | bytes 540672
  204.3 372.8 %reduce-scatter.19.cloned.1.call-start = ((), (), s32[]{:S(2)}) async-start(), calls=%async_computation.9 | async-start | bytes 540672 | tf_op jit(solution)/shard_map/reduce_scatter | solution.py:134
  205.7 460.9 %reduce-scatter.23.cloned.1.call-start = ((), (), s32[]{:S(2)}) async-start(), calls=%async_computation.11 | async-start | bytes 540672 | tf_op jit(solution)/shard_map/reduce_scatter | solution.py:137
  208.5 547.7 %reduce-scatter.17.cloned.1.call-start = ((), (), s32[]{:S(2)}) async-start(), calls=%async_computation.8 | async-start | bytes 540672 | tf_op jit(solution)/shard_map/reduce_scatter | solution.py:134
  209.9 635.9 %reduce-scatter.21.cloned.1.call-start = ((), (), s32[]{:S(2)}) async-start(), calls=%async_computation.10 | async-start | bytes 540672 | tf_op jit(solution)/shard_map/reduce_scatter | solution.py:137
  212.8 719.0 %all-reduce.6.cloned.1.call-start = ((), (), s32[]{:S(2)}) async-start(), calls=%async_computation.16 | async-start | bytes 1181696 | tf_op jit(solution)/shard_map/psum | solution.py:145
  (43 other events, 319.6 us)
Sparse Core Ops, SparseCore 0:
  128.0 91.0 reduce-scatter.30
  222.8 85.7 reduce-scatter.26
  312.4 85.8 reduce-scatter.28
  401.9 85.8 reduce-scatter.24
  491.3 85.8 reduce-scatter.18
  580.8 85.8 reduce-scatter.22
  670.3 85.8 reduce-scatter.16
  760.0 85.8 reduce-scatter.20
  849.9 81.7 all-reduce.5
where the time goes:
time: 949 us; the launch traced here: 947 us
  waiting for transfers between devices  665 us (70%)
  local copies, waits for them, and re-layouts  65.2 us (7%)
  matrix products  62.9 us (7%)
  blocking collectives  60.2 us (6%)
  starting transfers between devices  58 us (6%)
  other arithmetic  20.5 us (2%)
  between operations  15.5 us (2%)
    unnamed x13, waiting for transfers between devices  205 us
    reduce_scatter x2, waiting for transfers between devices, reduce_grads(): lax.psum_scatter(parts[3].astype(jnp.bfloat16), 'space', scatter_dimensio...  179 us
    reduce_scatter x2, waiting for transfers between devices, reduce_grads(): lax.psum_scatter(parts[2].astype(jnp.bfloat16), 'space', scatter_dimensio...  178 us
    psum x1, waiting for transfers between devices, reduce_grads(): lax.psum(shares[0].astype(jnp.bfloat16), 'slab').astype(jnp.float32)  82.8 us
    unnamed x1, blocking collectives  60.2 us
    ppermute x16, starting transfers between devices, shifted(): return lax.ppermute(block, axis, route)  57.4 us
    unnamed x103, local copies, waits for them, and re-layouts  25.9 us
    ppermute x16, waiting for transfers between devices, shifted(): return lax.ppermute(block, axis, route)  20 us
  transfers between devices with their start and end apart: 25, of which 14 were waited for; matrix products, arithmetic and copies ran while one was open for 8% of the time, Pallas kernels for 0%

commit v1 on v0

v1 whole, which is shorter than its diff:
```python
import jax
import jax.numpy as jnp
from jax import lax
from jax.experimental import pallas as pl
from jax.experimental.pallas import tpu as pltpu
from jax.sharding import PartitionSpec as P

EPS = 1e-05
BF = jnp.bfloat16
F32 = jnp.float32
MESH = pl.DeviceIdType.MESH

W = 512
BLOCK = 128
OWN = 4
TILES = 6
SLOTS = 12
ROWS = OWN * BLOCK
COLS = SLOTS * BLOCK
LAYERS = 2
NY, NZH, NCORE = 4, 4, 2
NX, NZL = 4, 2
NZ = NZH * NZL
N_SPACE = NY * NZH * NCORE
N_SLAB = NX * NZL
SHARE = W // N_SPACE

BUNDLE_TILES = (4, 5, 1)
CHUNK = 64


def sigmoid(v):
    return 0.5 * jnp.tanh(0.5 * v) + 0.5


def dot(a, b, ca, cb):
    return lax.dot_general(a, b, (((ca,), (cb,)), ((), ())), preferred_element_type=F32)


def loop(count, body):
    def step(i, carry):
        body(i)
        return carry

    lax.fori_loop(0, count, step, 0)


def rows_of(i, size):
    return pl.ds(pl.multiple_of(i * size, size), size)


class Bundle:
    def __init__(self, refs, place):
        (self.grad, self.held, self.y1, self.y2, self.x1, self.x2, self.z, self.full,
         self.send, self.recv) = refs
        self.place = place
        self.next = 0

    def copy(self, src, dst, device):
        i = self.next
        self.next += 1
        c = pltpu.make_async_remote_copy(
            src_ref=src, dst_ref=dst, send_sem=self.send.at[i], recv_sem=self.recv.at[i],
            device_id=device, device_id_type=MESH,
        )
        c.start()
        return c

    def add(self, dst, *others):
        total = dst[...].astype(F32)
        for other in others:
            total = total + other[...].astype(F32)
        dst[...] = total.astype(BF)

    def core_start(self):
        core = self.place["core"]
        self.core_copy = self.copy(self.grad.at[1 - core], self.held, self.place["at"](core=1 - core))

    def core_done(self):
        core = self.place["core"]
        self.core_copy.wait()

        def body(i):
            a, b = i // NX, i % NX
            self.held[a, b] = (
                self.held[a, b].astype(F32) + self.grad[core, a, b].astype(F32)
            ).astype(BF)

        loop(NY * NX, body)

    def halving_start(self, axis):
        me = self.place[axis]
        self.axis = axis
        if axis == "y":
            self.view = lambda i, half: self.held.at[i, :, pl.ds(2 * half, 2)]
            self.one, self.two = self.y1, self.y2
        else:
            self.view = lambda i, half: self.held.at[self.place["y"], i, pl.ds(2 * half, 2)]
            self.one, self.two = self.x1, self.x2
        near, far, cross = me ^ 1, me ^ 3, me ^ 2
        at = self.place["at"]
        self.step_one = [
            self.copy(self.view(cross, 0), self.one.at[0, 1], at(**{axis: near})),
            self.copy(self.view(cross, 1), self.one.at[1, 1], at(**{axis: far})),
            self.copy(self.view(near, 0), self.one.at[0, 0], at(**{axis: near})),
            self.copy(self.view(far, 1), self.one.at[1, 0], at(**{axis: far})),
        ]

    def halving_middle(self):
        me = self.place[self.axis]
        near, far = me ^ 1, me ^ 3
        at = self.place["at"]
        self.step_one[0].wait()
        self.add(self.view(far, 0), self.one.at[0, 1])
        self.step_two = [self.copy(self.view(far, 0), self.two.at[0], at(**{self.axis: far}))]
        self.step_one[1].wait()
        self.add(self.view(near, 1), self.one.at[1, 1])
        self.step_two.append(self.copy(self.view(near, 1), self.two.at[1], at(**{self.axis: near})))

    def halving_done(self):
        me = self.place[self.axis]
        self.step_one[2].wait()
        self.step_one[3].wait()
        for half in range(2):
            self.step_two[half].wait()
            self.add(self.view(me, half), self.one.at[half, 0], self.two.at[half])

    def z_start(self):
        place = self.place
        z = place["zh"] * NZL + place["zl"]
        self.z_copies = []
        for j in range(1, NZ):
            there = lax.rem(z + j, NZ)
            zh, zl = there // NZL, lax.rem(there, NZL)
            self.z_copies.append(
                self.copy(self.held.at[place["y"], place["x"], zh], self.z.at[j - 1], place["at"](zh=zh, zl=zl))
            )

    def z_done(self):
        place = self.place
        total = self.held[place["y"], place["x"], place["zh"]].astype(F32)
        for j, c in enumerate(self.z_copies):
            c.wait()
            total = total + self.z[j].astype(F32)
        self.full[place["x"]] = total.astype(BF)

    def gather_start(self):
        place = self.place
        mine = self.full.at[place["x"]]
        self.gather_copies = [
            self.copy(mine, mine, place["at"](x=lax.rem(place["x"] + j, NX))) for j in range(1, NX)
        ]

    def gather_done(self):
        for c in self.gather_copies:
            c.wait()

    def matrix(self, tile):
        return [self.full[q, :, tile * 128 : (tile + 1) * 128].astype(F32) for q in range(NX)]


N_COPIES = 1 + 6 + 6 + (NZ - 1) + (NX - 1)


def bundle_scratch(tiles):
    c = tiles * 128
    return [
        pltpu.VMEM((NCORE, NY, NX, NZH, SHARE, c), BF),
        pltpu.VMEM((NY, NX, NZH, SHARE, c), BF),
        pltpu.VMEM((2, 2, NX, 2, SHARE, c), BF),
        pltpu.VMEM((2, NX, 2, SHARE, c), BF),
        pltpu.VMEM((2, 2, 2, SHARE, c), BF),
        pltpu.VMEM((2, 2, SHARE, c), BF),
        pltpu.VMEM((NZ - 1, SHARE, c), BF),
        pltpu.VMEM((NX, SHARE, c), BF),
        pltpu.SemaphoreType.DMA((N_COPIES,)),
        pltpu.SemaphoreType.DMA((N_COPIES,)),
    ]


def kernel(
    lat_in, up_in, wm_in, ws_in, wa_in, wo_in, gains, edge_in, nbr, sends,
    lat_out, grad_out, gm_out, gs_out, ga_out, go_out, gg_out,
    xs, up, wm, ws, wa, wo, edge, adj, own, ext, out_blocks, back, ret,
    pm, ph, normed, inverse, merged, hidden, acc, acc2, gy, gu, gph, gmg, gpm, in_sem, out_sem,
    halo_send, halo_recv, *bundle_refs,
):
    space = lax.axis_index("space")
    slab = lax.axis_index("slab")
    core = lax.rem(space, NCORE)
    zh = lax.rem(space // NCORE, NZH)
    y = space // (NCORE * NZH)
    zl = lax.rem(slab, NZL)
    x = slab // NZL

    def at(**new):
        p = {"core": core, "zh": zh, "y": y, "zl": zl, "x": x, **new}
        return ((p["y"] * NZH + p["zh"]) * NCORE + p["core"], p["x"] * NZL + p["zl"])

    place = {"core": core, "zh": zh, "y": y, "zl": zl, "x": x, "at": at}
    s_up, s_down = lax.rem(space + 1, N_SPACE), lax.rem(space + N_SPACE - 1, N_SPACE)
    l_up, l_down = lax.rem(slab + 1, N_SLAB), lax.rem(slab + N_SLAB - 1, N_SLAB)
    ahead = [(s_up, slab), (s_down, slab), (space, l_up), (space, l_down)]
    behind = [ahead[1], ahead[0], ahead[3], ahead[2]]

    pairs = [
        (lat_in, xs.at[0]), (wm_in, wm), (ws_in, ws), (edge_in, edge), (wa_in, wa), (wo_in, wo), (up_in, up),
    ]
    loads = [pltpu.make_async_copy(a, b, in_sem.at[i]) for i, (a, b) in enumerate(pairs)]
    for c in loads:
        c.start()
    lat_load, wm_load, ws_load, edge_load, wa_load, wo_load, up_load = loads

    barrier = pltpu.get_barrier_semaphore()
    partners = list(ahead) + [at(core=1 - core), at(y=y ^ 1), at(y=y ^ 3)]
    partners += [at(x=lax.rem(x + j, NX)) for j in range(1, NX)]
    z = zh * NZL + zl
    for j in range(1, NZ):
        there = lax.rem(z + j, NZ)
        partners.append(at(zh=there // NZL, zl=lax.rem(there, NZL)))
    for p in partners:
        pl.semaphore_signal(barrier, inc=1, device_id=p, device_id_type=MESH)

    count = len(bundle_refs) // len(BUNDLE_TILES)
    bundles = [Bundle(bundle_refs[i * count : (i + 1) * count], place) for i in range(len(BUNDLE_TILES))]

    def matmul(out, a, b, ca, cb):
        def body(i):
            r = rows_of(i, 256)
            out[r] = dot(a[r] if ca == 1 else a[:, r], b[...], ca, cb)

        loop(ROWS // 256, body)

    def matmul_add(out, a, b, ca, cb):
        def body(i):
            r = rows_of(i, 256)
            out[r] = out[r] + dot(a[r] if ca == 1 else a[:, r], b[...], ca, cb)

        loop(ROWS // 256, body)

    def halo(src, dst, peers, exchange):
        copies = []
        for d in range(4):
            c = pltpu.make_async_remote_copy(
                src_ref=src(d), dst_ref=dst(d), send_sem=halo_send.at[exchange, d],
                recv_sem=halo_recv.at[exchange, d], device_id=peers[d], device_id_type=MESH,
            )
            c.start()
            copies.append(c)
        return copies

    for l in range(LAYERS):
        if l == 0:
            lat_load.wait()
            wm_load.wait()
        matmul(pm.at[l], xs.at[l], wm.at[l], 1, 0)

        def silu_message(i, l=l):
            v = pm[l, rows_of(i, CHUNK)]
            own[l, i // 2, rows_of(lax.rem(i, 2), CHUNK)] = (v * sigmoid(v)).astype(BF)

        loop(ROWS // CHUNK, silu_message)
        for d in range(4):
            for t in range(2):
                out_blocks[l, d, t] = own[l, sends[d, t]]
        if l == 0:
            pl.semaphore_wait(barrier, len(partners))
        copies = halo(
            lambda d: out_blocks.at[l, d], lambda d: ext.at[l, d], ahead, l
        )
        if l == 0:
            edge_load.wait()

            def build(i):
                b = i // SLOTS
                e = lax.rem(i, SLOTS)
                total = jnp.zeros((BLOCK, BLOCK), F32)
                for k in range(TILES):
                    keep = jnp.where(nbr[b, k] == e, 1.0, 0.0)
                    total = total + edge[b, k].astype(F32) * keep
                adj[e, rows_of(b, BLOCK), :] = total.astype(BF)

            loop(OWN * SLOTS, build)
            ws_load.wait()

        matmul(ph.at[l], xs.at[l], ws.at[l], 1, 0)

        def adjacency(e, blocks):
            return jnp.concatenate([adj[e + j] for j in range(blocks)], axis=1)

        acc[...] = dot(adjacency(0, OWN), own[l].reshape(ROWS, W), 1, 0)
        for d in range(4):
            copies[d].wait()
            acc[...] += dot(adjacency(OWN + 2 * d, 2), ext[l, d].reshape(2 * BLOCK, W), 1, 0)
        merged[l] = acc[...].astype(BF)
        if l == 0:
            wa_load.wait()
            wo_load.wait()
        matmul_add(ph.at[l], merged.at[l], wa.at[l], 1, 0)

        def silu_hidden(i, l=l):
            r = rows_of(i, CHUNK)
            v = ph[l, r]
            hidden[l, r] = (v * sigmoid(v)).astype(BF)

        loop(ROWS // CHUNK, silu_hidden)
        matmul(acc, hidden.at[l], wo.at[l], 1, 0)

        def norm(i, l=l):
            r = rows_of(i, CHUNK)
            u = acc[r]
            centred = u - jnp.mean(u, axis=-1, keepdims=True)
            inv = lax.rsqrt(jnp.mean(centred * centred, axis=-1, keepdims=True) + EPS)
            n = centred * inv
            normed[l, r] = n
            inverse[l, r] = inv
            xs[l + 1, r] = (xs[l, r].astype(F32) + gains[l : l + 1, :] * n).astype(BF)

        loop(ROWS // CHUNK, norm)

    out_copy = pltpu.make_async_copy(xs.at[LAYERS], lat_out, out_sem.at[0])
    out_copy.start()

    def weight_grad(bundle, tile, a, g):
        for i in range(2):
            r = pl.ds(i * 256, 256)
            v = dot(a[:, r], g[...], 0, 0).astype(BF).reshape(2, NZH, NCORE, SHARE, W)
            for c in range(NCORE):
                for q in range(NX):
                    bundle.grad[c, pl.ds(2 * i, 2), q, :, :, tile * 128 : (tile + 1) * 128] = v[
                        :, :, c, :, q * 128 : (q + 1) * 128
                    ]

    def gain_grad(bundle, tile, row):
        v = jnp.transpose(jnp.broadcast_to(row, (128, W))).astype(BF).reshape(NY, NZH, NCORE, SHARE, 128)
        for c in range(NCORE):
            for q in range(NX):
                bundle.grad[c, :, q, :, :, tile * 128 : (tile + 1) * 128] = v[:, :, c]

    for l in reversed(range(LAYERS)):
        if l == LAYERS - 1:
            up_load.wait()

            def start(i):
                r = rows_of(i, CHUNK)
                gy[r] = up[r].astype(F32)

            loop(ROWS // CHUNK, start)

        def norm_grad(i, row, l=l):
            r = rows_of(i, CHUNK)
            g = gy[r]
            n = normed[l, r]
            row = row + jnp.sum(g * n, axis=0, keepdims=True)
            g = g * gains[l : l + 1, :]
            u = g - jnp.mean(g, axis=-1, keepdims=True) - n * jnp.mean(g * n, axis=-1, keepdims=True)
            gu[r] = (inverse[l, r] * u).astype(BF)
            return row

        gain_row = lax.fori_loop(0, ROWS // CHUNK, norm_grad, jnp.zeros((1, W), F32))
        matmul(acc, gu, wo.at[l], 1, 1)

        def hidden_grad(i, l=l):
            r = rows_of(i, CHUNK)
            v = ph[l, r]
            s = sigmoid(v)
            gph[l, r] = (acc[r] * (s * (1.0 + v * (1.0 - s)))).astype(BF)

        loop(ROWS // CHUNK, hidden_grad)
        matmul(acc, gph.at[l], wa.at[l], 1, 1)
        gmg[...] = acc[...].astype(BF)
        for e in range(OWN, SLOTS):
            back[l, (e - OWN) // 2, (e - OWN) % 2] = dot(adj[e], gmg[...], 0, 0).astype(BF)
        copies = halo(lambda d: back.at[l, d], lambda d: ret.at[l, d], behind, LAYERS + l)

        bundle = bundles[LAYERS - 1 - l]
        t = 0
        if l == 0:
            weight_grad(bundle, 0, xs.at[1], gpm)
            t = 1
        weight_grad(bundle, t, hidden.at[l], gu)
        weight_grad(bundle, t + 1, xs.at[l], gph.at[l])
        weight_grad(bundle, t + 2, merged.at[l], gph.at[l])
        gain_grad(bundle, t + 3, gain_row)
        bundle.core_start()
        for e in range(OWN):
            acc2[e * BLOCK : (e + 1) * BLOCK] = dot(adj[e], gmg[...], 0, 0)
        matmul_add(gy, gph.at[l], ws.at[l], 1, 1)
        bundle.core_done()
        bundle.halving_start("y")
        bundle.halving_middle()
        bundle.halving_done()
        bundle.halving_start("x")
        bundle.halving_middle()
        bundle.halving_done()
        bundle.z_start()
        for c in copies:
            c.wait()

        def message_grad(i, l=l):
            b = i // 2
            r = rows_of(i, CHUNK)
            inner = rows_of(lax.rem(i, 2), CHUNK)
            total = acc2[r]
            for d in range(4):
                for t in range(2):
                    keep = jnp.where(sends[d, t] == b, 1.0, 0.0)
                    total = total + ret[l, d, t, inner].astype(F32) * keep
            v = pm[l, r]
            s = sigmoid(v)
            gpm[r] = (total * (s * (1.0 + v * (1.0 - s)))).astype(BF)

        loop(ROWS // CHUNK, message_grad)
        if l == 0:
            weight_grad(bundles[2], 0, xs.at[0], gpm)
            bundles[2].core_start()
        matmul_add(gy, gpm, wm.at[l], 1, 1)

    grad_copy = pltpu.make_async_copy(gy, grad_out, out_sem.at[1])
    grad_copy.start()
    tail = bundles[2]
    tail.core_done()
    tail.halving_start("y")
    for bundle in bundles[:2]:
        bundle.z_done()
        bundle.gather_start()
    tail.halving_middle()
    tail.halving_done()
    tail.halving_start("x")
    tail.halving_middle()
    tail.halving_done()
    tail.z_start()
    for bundle in bundles[:2]:
        bundle.gather_done()
    tail.z_done()
    tail.gather_start()

    def put(out, l, bundle, tile):
        for q, v in enumerate(bundle.matrix(tile)):
            out[l, :, q * 128 : (q + 1) * 128] = v

    def put_gain(l, bundle, tile):
        v = bundle.matrix(tile)[0]
        same = lax.broadcasted_iota(jnp.int32, v.shape, 0) == lax.broadcasted_iota(jnp.int32, v.shape, 1)
        gg_out[l : l + 1, :] = jnp.sum(jnp.where(same, v, 0.0), axis=0, keepdims=True)[:, :SHARE]

    put(go_out, 1, bundles[0], 0)
    put(gs_out, 1, bundles[0], 1)
    put(ga_out, 1, bundles[0], 2)
    put_gain(1, bundles[0], 3)
    put(gm_out, 1, bundles[1], 0)
    put(go_out, 0, bundles[1], 1)
    put(gs_out, 0, bundles[1], 2)
    put(ga_out, 0, bundles[1], 3)
    put_gain(0, bundles[1], 4)
    tail.gather_done()
    put(gm_out, 0, tail, 0)
    out_copy.wait()
    grad_copy.wait()


def local(
    latents, upstream, msg_weight, self_weight, agg_weight, out_weight, gains, edge_weight, nbr_slot, send_list
):
    sends = send_list.reshape(4, send_list.shape[-1])
    hbm = pl.BlockSpec(memory_space=pl.ANY)
    vmem = pl.BlockSpec(memory_space=pltpu.VMEM)
    smem = pl.BlockSpec(memory_space=pltpu.SMEM)
    share = jax.ShapeDtypeStruct((LAYERS, SHARE, W), F32)
    scratch = [
        pltpu.VMEM((LAYERS + 1, ROWS, W), BF),
        pltpu.VMEM((ROWS, W), BF),
        pltpu.VMEM((LAYERS, W, W), BF),
        pltpu.VMEM((LAYERS, W, W), BF),
        pltpu.VMEM((LAYERS, W, W), BF),
        pltpu.VMEM((LAYERS, W, W), BF),
        pltpu.VMEM((OWN, TILES, BLOCK, BLOCK), BF),
        pltpu.VMEM((SLOTS, ROWS, BLOCK), BF),
        pltpu.VMEM((LAYERS, OWN, BLOCK, W), BF),
        pltpu.VMEM((LAYERS, 4, 2, BLOCK, W), BF),
        pltpu.VMEM((LAYERS, 4, 2, BLOCK, W), BF),
        pltpu.VMEM((LAYERS, 4, 2, BLOCK, W), BF),
        pltpu.VMEM((LAYERS, 4, 2, BLOCK, W), BF),
        pltpu.VMEM((LAYERS, ROWS, W), F32),
        pltpu.VMEM((LAYERS, ROWS, W), F32),
        pltpu.VMEM((LAYERS, ROWS, W), F32),
        pltpu.VMEM((LAYERS, ROWS, 1), F32),
        pltpu.VMEM((LAYERS, ROWS, W), BF),
        pltpu.VMEM((LAYERS, ROWS, W), BF),
        pltpu.VMEM((ROWS, W), F32),
        pltpu.VMEM((ROWS, W), F32),
        pltpu.VMEM((ROWS, W), F32),
        pltpu.VMEM((ROWS, W), BF),
        pltpu.VMEM((LAYERS, ROWS, W), BF),
        pltpu.VMEM((ROWS, W), BF),
        pltpu.VMEM((ROWS, W), BF),
        pltpu.SemaphoreType.DMA((7,)),
        pltpu.SemaphoreType.DMA((2,)),
        pltpu.SemaphoreType.DMA((2 * LAYERS, 4)),
        pltpu.SemaphoreType.DMA((2 * LAYERS, 4)),
    ]
    for tiles in BUNDLE_TILES:
        scratch += bundle_scratch(tiles)
    out = pl.pallas_call(
        kernel,
        out_shape=(
            jax.ShapeDtypeStruct((ROWS, W), BF),
            jax.ShapeDtypeStruct((ROWS, W), F32),
            share, share, share, share,
            jax.ShapeDtypeStruct((LAYERS, SHARE), F32),
        ),
        in_specs=[hbm, hbm, hbm, hbm, hbm, hbm, vmem, hbm, smem, smem],
        out_specs=(hbm, hbm, vmem, vmem, vmem, vmem, vmem),
        scratch_shapes=scratch,
        compiler_params=pltpu.CompilerParams(
            collective_id=0, has_side_effects=True, vmem_limit_bytes=60 * 1024 * 1024
        ),
        cost_estimate=pl.CostEstimate(flops=10 * 10**9, bytes_accessed=10 * 2**20, transcendentals=2 * 10**6),
    )(latents, upstream, msg_weight, self_weight, agg_weight, out_weight, gains, edge_weight, nbr_slot, sends)
    return out


def solution(mesh):
    rows = P(("space", "slab"), None)
    return jax.shard_map(
        local,
        mesh=mesh,
        in_specs=(
            rows, rows, P(), P(), P(), P(), P(),
            P(("space", "slab"), None, None, None), rows, P("space", "slab", None, None),
        ),
        out_specs=(
            rows, rows, P(None, "space", None), P(None, "space", None), P(None, "space", None),
            P(None, "space", None), P(None, "space"),
        ),
        check_vma=False,
    )
```

time: 949 us -> 146 us (0.15)
  waiting for transfers between devices: 665 us -> 0 us
  Pallas kernels: 0 us -> 136 us
  matrix products: 62.9 us -> 0 us
  blocking collectives: 60.2 us -> 0 us
  starting transfers between devices: 58 us -> 0 us
  local copies, waits for them, and re-layouts: 65.2 us -> 8.09 us
  other arithmetic: 20.5 us -> 0 us
  between operations: 15.5 us -> 0.67 us
    reduce_scatter x4 -> x0, waiting for transfers between devices: 357 us -> none  [the longest x2 179 us: reduce_grads(): lax.psum_scatter(parts[3].astype(jnp.bfloat16), 'space', scatter_dimensio...]
    unnamed x13 -> x0, waiting for transfers between devices: 205 us -> none
    pallas_call x0 -> x1, Pallas kernels: none -> 136 us  [local(): pl.pallas_call(kernel, out_shape=(jax.ShapeDtypeStruct((ROWS, W), BF), ja...]
    psum x1 -> x0, waiting for transfers between devices: 82.8 us -> none  [reduce_grads(): lax.psum(shares[0].astype(jnp.bfloat16), 'slab').astype(jnp.float32)]
    dot_general x38 -> x0, matrix products: 62.9 us -> none  [the longest x2 14.9 us: backward_layer(): jnp.einsum('ce,cjw->ejw', chooser, contrib, precision=lax.Precision.HIGHEST)]
    unnamed x1 -> x0, blocking collectives: 60.2 us -> none
    ppermute x16 -> x0, starting transfers between devices: 57.4 us -> none  [shifted(): return lax.ppermute(block, axis, route)]
    ppermute x16 -> x0, waiting for transfers between devices: 20 us -> none  [shifted(): return lax.ppermute(block, axis, route)]
  transfers between devices with their start and end apart: 25 -> 0, of which waited for: 14 -> 0; matrix products, arithmetic and copies ran while one was open for 8% -> 0% of each run, Pallas kernels for 0% -> 0%
where the time goes in v1:
time: 146 us; the launch traced here: 145 us
  Pallas kernels  136 us (93%)
  local copies, waits for them, and re-layouts  8.09 us (6%)
    pallas_call x1, Pallas kernels, local(): pl.pallas_call(kernel, out_shape=(jax.ShapeDtypeStruct((ROWS, W), BF), ja...  136 us
    unnamed x21, local copies, waits for them, and re-layouts  7.43 us

profile of v1, /device:TPU:8, one launch (start us, length us, event | category | flops | bytes accessed | tf_op | source)
XLA Modules:
  0.0 144.8 jit_solution(18060813305572226889)
XLA Ops:
  0.6 0.0 copy-start.5
  0.6 0.7 copy-done.5
  1.3 0.7 copy.17.sends
  2.0 136.0 %shard_map.153 = (bf16[512,512]{1,0:T(8,128)(2,1)}, f32[512,512]{1,0:T(8,128)}, f32[2,16,512]{2,1,0:T(8,128)}, f32[2,16,512]{2,1,0:T(8,128)}, f32[2,16,512]{2,1,...) custom-call(bf16[512,512]{1,0:T(8,128)(2,1)} %lat_in.1, bf16[512,512]{1,0:T(8,128)(2,1)} %up_in.1, ...), custom_call_target="tpu_custom_call" | custom-call | flops 10000000000 | bytes 10485760 | tf_op jit(solution)/shard_map/pallas_call | solution.py:504
  138.0 0.0 copy-start
  138.0 2.0 %copy.25 = bf16[512,512]{1,0:T(8,128)(2,1)} copy(bf16[512,512]{1,0:T(8,128)(2,1)} %get-tuple-element.14) | data formatting | bytes 1048576
  140.0 0.0 copy-done
  140.0 0.0 copy-start.4
  140.0 1.0 copy.26
  140.9 0.0 copy-done.4
  140.9 0.0 copy-start.3
  140.9 0.6 copy.27
  141.6 0.2 copy-done.3
  141.8 0.0 copy-start.2
  141.8 0.6 copy.28
  142.4 0.2 copy-done.2
  142.7 0.0 copy-start.1
  142.7 0.6 copy.29
  143.3 0.2 copy-done.1
  143.5 0.0 copy-start.6
  143.5 0.6 copy.30
  144.2 0.0 copy-done.6
  144.2 0.6 copy.31
Async XLA Ops:
  0.6 0.7 copy-start.5
  138.0 2.0 %copy-start = (f32[512,512]{1,0:T(8,128)S(1)}, f32[512,512]{1,0:T(8,128)}, u32[]{:S(2)}) copy-start(f32[512,512]{1,0:T(8,128)} %get-tuple-element.15) | copy-start | bytes 3145732
  140.0 1.0 copy-start.4
  140.9 0.9 copy-start.3
  141.8 0.9 copy-start.2
  142.7 0.9 copy-start.1
  143.5 0.7 copy-start.6

commit v2 on v1

v2 whole, which is shorter than its diff:
```python
import jax
import jax.numpy as jnp
from jax import lax
from jax.experimental import pallas as pl
from jax.experimental.pallas import tpu as pltpu
from jax.sharding import PartitionSpec as P

EPS = 1e-05
BF = jnp.bfloat16
F32 = jnp.float32
MESH = pl.DeviceIdType.MESH

W = 512
BLOCK = 128
OWN = 4
TILES = 6
SLOTS = 12
ROWS = OWN * BLOCK
COLS = SLOTS * BLOCK
LAYERS = 2
NY, NZH, NCORE = 4, 4, 2
NX, NZL = 4, 2
NZ = NZH * NZL
N_SPACE = NY * NZH * NCORE
N_SLAB = NX * NZL
SHARE = W // N_SPACE

BUNDLE_TILES = (4, 5, 1)
PARTS = NZH


def sigmoid(v):
    return 0.5 * jnp.tanh(0.5 * v) + 0.5


def slope(v, s):
    return s * (1.0 + v * (1.0 - s))


def dot(a, b, ca, cb):
    return lax.dot_general(a, b, (((ca,), (cb,)), ((), ())), preferred_element_type=F32)


def loop(count, body):
    def step(i, carry):
        body(i)
        return carry

    lax.fori_loop(0, count, step, 0)


def rows_of(i, size):
    return pl.ds(pl.multiple_of(i * size, size), size)


def block_rows(b):
    return slice(b * BLOCK, (b + 1) * BLOCK)


def add(dst, *others):
    total = dst[...].astype(F32)
    for other in others:
        total = total + other[...].astype(F32)
    dst[...] = total.astype(BF)


class Bundle:
    def __init__(self, refs, place):
        self.grad, self.held, self.z, self.full, self.send, self.recv, *self.more = refs
        self.place = place
        self.next = 0

    def copy(self, src, dst, device):
        i = self.next
        self.next += 1
        c = pltpu.make_async_remote_copy(
            src_ref=src, dst_ref=dst, send_sem=self.send.at[i], recv_sem=self.recv.at[i],
            device_id=device, device_id_type=MESH,
        )
        c.start()
        return c

    def core_start(self):
        core = self.place["core"]
        self.core_copy = self.copy(self.grad.at[1 - core], self.held, self.place["at"](core=1 - core))

    def core_done(self):
        core = self.place["core"]
        self.core_copy.wait()

        def body(i):
            self.held[i] = (self.held[i].astype(F32) + self.grad[core, i].astype(F32)).astype(BF)

        loop(NY, body)

    def z_start(self):
        place = self.place
        z = place["zh"] * NZL + place["zl"]
        self.z_copies = []
        for j in range(1, NZ):
            there = lax.rem(z + j, NZ)
            zh, zl = there // NZL, lax.rem(there, NZL)
            self.z_copies.append(
                self.copy(self.held.at[place["y"], place["x"], zh], self.z.at[j - 1], place["at"](zh=zh, zl=zl))
            )

    def z_done(self):
        place = self.place
        total = self.held[place["y"], place["x"], place["zh"]].astype(F32)
        for j, c in enumerate(self.z_copies):
            c.wait()
            total = total + self.z[j].astype(F32)
        self.full[place["x"]] = total.astype(BF)

    def gather_start(self):
        place = self.place
        mine = self.full.at[place["x"]]
        self.gather_copies = [
            self.copy(mine, mine, place["at"](x=lax.rem(place["x"] + j, NX))) for j in range(1, NX)
        ]

    def gather_done(self):
        for c in self.gather_copies:
            c.wait()

    def matrix(self, tile):
        return [self.full[q, :, tile * 128 : (tile + 1) * 128].astype(F32) for q in range(NX)]


class Halving(Bundle):
    def setup(self):
        self.first = []
        self.second = []
        for p in range(PARTS):
            axes = ("y", "x") if p < PARTS // 2 else ("x", "y")
            near, far = (1, 3) if p % 2 == 0 else (3, 1)
            self.first.append((axes[0], near, far))
            self.second.append((axes[1], near, far))

    def view(self, p, stage, i):
        axis = (self.first if stage == 0 else self.second)[p][0]
        y, x = self.place["y"], self.place["x"]
        if stage == 0:
            return self.held.at[i, :, p] if axis == "y" else self.held.at[:, i, p]
        return self.held.at[i, x, p] if axis == "y" else self.held.at[y, i, p]

    def pairs_start(self, stage):
        self.setup()
        land = self.more[2 * stage]
        at = self.place["at"]
        self.cross, self.near, self.far = [], [], []
        for slot in (1, 0):
            for p, (axis, near, _) in enumerate((self.first, self.second)[stage]):
                me = self.place[axis]
                chunk = me ^ 2 if slot else me ^ near
                c = self.copy(self.view(p, stage, chunk), land.at[p, slot], at(**{axis: me ^ near}))
                (self.cross if slot else self.near).append(c)

    def pairs_middle(self, stage):
        land, land_two = self.more[2 * stage], self.more[2 * stage + 1]
        at = self.place["at"]
        for p, (axis, near, far) in enumerate((self.first, self.second)[stage]):
            me = self.place[axis]
            self.cross[p].wait()
            chunk = self.view(p, stage, me ^ far)
            add(chunk, land.at[p, 1])
            self.far.append(self.copy(chunk, land_two.at[p], at(**{axis: me ^ far})))

    def pairs_done(self, stage):
        land, land_two = self.more[2 * stage], self.more[2 * stage + 1]
        for p, (axis, near, far) in enumerate((self.first, self.second)[stage]):
            self.near[p].wait()
            self.far[p].wait()
            add(self.view(p, stage, self.place[axis]), land.at[p, 0], land_two.at[p])


class Direct(Bundle):
    def plane_start(self):
        place = self.place
        (land,) = self.more
        self.plane = []
        for i in range(NY):
            for j in range(NX):
                if i or j:
                    y, x = lax.rem(place["y"] + i, NY), lax.rem(place["x"] + j, NX)
                    self.plane.append(
                        self.copy(self.held.at[y, x], land.at[len(self.plane)], place["at"](y=y, x=x))
                    )

    def plane_done(self):
        (land,) = self.more
        y, x = self.place["y"], self.place["x"]
        for c in self.plane:
            c.wait()
        total = self.held[y, x].astype(F32)
        for j in range(NY * NX - 1):
            total = total + land[j].astype(F32)
        self.held[y, x] = total.astype(BF)


def bundle_scratch(tiles, direct):
    c = tiles * 128
    copies = 1 + (NZ - 1) + (NX - 1) + (NY * NX - 1 if direct else 6 * PARTS)
    refs = [
        pltpu.VMEM((NCORE, NY, NX, NZH, SHARE, c), BF),
        pltpu.VMEM((NY, NX, NZH, SHARE, c), BF),
        pltpu.VMEM((NZ - 1, SHARE, c), BF),
        pltpu.VMEM((NX, SHARE, c), BF),
        pltpu.SemaphoreType.DMA((copies,)),
        pltpu.SemaphoreType.DMA((copies,)),
    ]
    if direct:
        return refs + [pltpu.VMEM((NY * NX - 1, NZH, SHARE, c), BF)]
    return refs + [
        pltpu.VMEM((PARTS, 2, 4, SHARE, c), BF),
        pltpu.VMEM((PARTS, 4, SHARE, c), BF),
        pltpu.VMEM((PARTS, 2, SHARE, c), BF),
        pltpu.VMEM((PARTS, SHARE, c), BF),
    ]


def kernel(
    lat_in, up_in, wm_in, ws_in, wa_in, wo_in, gains_in, edge_in, nbr_in, sends_in,
    lat_out, grad_out, gm_out, gs_out, ga_out, go_out, gg_out,
    xs, up, wm, ws, wa, wo, gains, edge, nbr, sends, adj, own, ext, out_blocks, back, ret0, ret1,
    pm, ph, normed, inverse, merged, hidden, acc, acc2, gy, gu, gph, gmg, gpm, in_sem, out_sem,
    halo_send, halo_recv, *bundle_refs,
):
    space = lax.axis_index("space")
    slab = lax.axis_index("slab")
    core = lax.rem(space, NCORE)
    zh = lax.rem(space // NCORE, NZH)
    y = space // (NCORE * NZH)
    zl = lax.rem(slab, NZL)
    x = slab // NZL

    def at(**new):
        p = {"core": core, "zh": zh, "y": y, "zl": zl, "x": x, **new}
        return ((p["y"] * NZH + p["zh"]) * NCORE + p["core"], p["x"] * NZL + p["zl"])

    place = {"core": core, "zh": zh, "y": y, "zl": zl, "x": x, "at": at}
    s_up, s_down = lax.rem(space + 1, N_SPACE), lax.rem(space + N_SPACE - 1, N_SPACE)
    l_up, l_down = lax.rem(slab + 1, N_SLAB), lax.rem(slab + N_SLAB - 1, N_SLAB)
    ahead = [(s_up, slab), (s_down, slab), (space, l_up), (space, l_down)]
    behind = [ahead[1], ahead[0], ahead[3], ahead[2]]

    barrier = pltpu.get_barrier_semaphore()
    partners = list(ahead) + [at(core=1 - core)]
    partners += [at(y=lax.rem(y + i, NY), x=lax.rem(x + j, NX)) for i in range(NY) for j in range(NX) if i or j]
    z = zh * NZL + zl
    for j in range(1, NZ):
        there = lax.rem(z + j, NZ)
        partners.append(at(zh=there // NZL, zl=lax.rem(there, NZL)))
    for p in partners:
        pl.semaphore_signal(barrier, inc=1, device_id=p, device_id_type=MESH)

    pairs = [
        (lat_in, xs.at[0]), (wm_in, wm), (sends_in.at[0, 0], sends), (nbr_in, nbr), (edge_in, edge), (ws_in, ws),
        (wa_in, wa), (wo_in, wo), (gains_in, gains), (up_in, up),
    ]
    loads = [pltpu.make_async_copy(a, b, in_sem.at[i]) for i, (a, b) in enumerate(pairs)]
    for c in loads:
        c.start()
    lat_load, wm_load, sends_load, nbr_load, edge_load, ws_load, wa_load, wo_load, gains_load, up_load = loads

    count = len(bundle_scratch(1, False))
    early = Halving(bundle_refs[:count], place)
    late = Halving(bundle_refs[count : 2 * count], place)
    tail = Direct(bundle_refs[2 * count :], place)
    ret = (ret0, ret1)

    def halo(src, dst, peers, exchange, before):
        copies = []
        for d in range(4):
            before(d)
            c = pltpu.make_async_remote_copy(
                src_ref=src(d), dst_ref=dst(d), send_sem=halo_send.at[exchange, d],
                recv_sem=halo_recv.at[exchange, d], device_id=peers[d], device_id_type=MESH,
            )
            c.start()
            copies.append(c)
        return copies

    def adjacency(e, blocks, rows=slice(None)):
        return jnp.concatenate([adj[e + j, rows] for j in range(blocks)], axis=1)

    def message(l, b, latent):
        v = dot(latent, wm[l], 1, 0)
        pm[l, block_rows(b)] = v
        own[l, b] = (v * sigmoid(v)).astype(BF)

    def gathered(l):
        def pick(d):
            for t in range(2):
                out_blocks[l, d, t] = own[l, sends[t, d]]

        return pick

    lat_load.wait()
    wm_load.wait()
    for b in range(OWN):
        message(0, b, xs[0, block_rows(b)])
    sends_load.wait()
    pl.semaphore_wait(barrier, len(partners))
    gain_row = jnp.zeros((1, W), F32)

    def update_grad(l, b, g, n, inv):
        r = block_rows(b)
        row = jnp.sum(g * n, axis=0, keepdims=True)
        g = g * gains[l : l + 1, :]
        u = g - jnp.mean(g, axis=-1, keepdims=True) - n * jnp.mean(g * n, axis=-1, keepdims=True)
        u = (inv * u).astype(BF)
        gu[l, r] = u
        h = (dot(u, wo[l], 1, 1) * ph[l, r]).astype(BF)
        gph[l, r] = h
        gmg[r] = dot(h, wa[l], 1, 1).astype(BF)
        return row

    for l in range(LAYERS):
        copies = halo(lambda d: out_blocks.at[l, d], lambda d: ext.at[l, d], ahead, l, gathered(l))
        if l == 0:
            edge_load.wait()
            nbr_load.wait()

            def build(i):
                b = i // SLOTS
                e = lax.rem(i, SLOTS)
                total = jnp.zeros((BLOCK, BLOCK), F32)
                for k in range(TILES):
                    keep = jnp.where(nbr[b, k] == e, 1.0, 0.0)
                    total = total + edge[b, k].astype(F32) * keep
                adj[e, rows_of(b, BLOCK), :] = total.astype(BF)

            loop(OWN * SLOTS, build)
            for c in (ws_load, wa_load, wo_load, gains_load, up_load):
                c.wait()
        for b in range(OWN):
            r = block_rows(b)
            ph[l, r] = dot(xs[l, r], ws[l], 1, 0)
            acc[r] = dot(adjacency(0, OWN, r), own[l].reshape(ROWS, W), 1, 0)
            v = pm[l, r]
            pm[l, r] = slope(v, sigmoid(v))
        for d in range(4):
            copies[d].wait()
            if d < 3:
                for b in range(OWN):
                    r = block_rows(b)
                    acc[r] += dot(adjacency(OWN + 2 * d, 2, r), ext[l, d].reshape(2 * BLOCK, W), 1, 0)
        for b in range(OWN):
            r = block_rows(b)
            m = (acc[r] + dot(adjacency(OWN + 6, 2, r), ext[l, 3].reshape(2 * BLOCK, W), 1, 0)).astype(BF)
            merged[l, r] = m
            v = ph[l, r] + dot(m, wa[l], 1, 0)
            s = sigmoid(v)
            h = (v * s).astype(BF)
            hidden[l, r] = h
            ph[l, r] = slope(v, s)
            u = dot(h, wo[l], 1, 0)
            centred = u - jnp.mean(u, axis=-1, keepdims=True)
            inv = lax.rsqrt(jnp.mean(centred * centred, axis=-1, keepdims=True) + EPS)
            n = centred * inv
            out = (xs[l, r].astype(F32) + gains[l : l + 1, :] * n).astype(BF)
            xs[l + 1, r] = out
            if l + 1 < LAYERS:
                normed[l, r] = n
                inverse[l, r] = inv
                message(l + 1, b, out)
            else:
                gain_row = gain_row + update_grad(l, b, up[r].astype(F32), n, inv)

    def weight_grad(bundle, tile, a, g):
        for i in range(2):
            r = pl.ds(i * 256, 256)
            v = dot(a[:, r], g[...], 0, 0).astype(BF).reshape(2, NZH, NCORE, SHARE, W)
            for c in range(NCORE):
                for q in range(NX):
                    bundle.grad[c, pl.ds(2 * i, 2), q, :, :, tile * 128 : (tile + 1) * 128] = v[
                        :, :, c, :, q * 128 : (q + 1) * 128
                    ]

    def gain_grad(bundle, tile, row):
        v = jnp.transpose(jnp.broadcast_to(row, (128, W))).astype(BF).reshape(NY, NZH, NCORE, SHARE, 128)
        for c in range(NCORE):
            for q in range(NX):
                bundle.grad[c, :, q, :, :, tile * 128 : (tile + 1) * 128] = v[:, :, c]

    for l in reversed(range(LAYERS)):

        def back_grad(d, l=l):
            v = dot(adjacency(OWN + 2 * d, 2), gmg[...], 0, 0)
            back[l, d] = v.astype(BF).reshape(2, BLOCK, W)

        copies = halo(lambda d: back.at[l, d], lambda d: ret[l].at[d, pl.ds(0, 2)], behind, LAYERS + l, back_grad)

        bundle = (late, early)[l]
        t = 0
        if l == 0:
            weight_grad(bundle, 0, xs.at[1], gpm.at[1])
            t = 1
        weight_grad(bundle, t, hidden.at[l], gu.at[l])
        weight_grad(bundle, t + 1, xs.at[l], gph.at[l])
        weight_grad(bundle, t + 2, merged.at[l], gph.at[l])
        gain_grad(bundle, t + 3, gain_row)
        bundle.core_start()
        for d in range(4):
            ret[l][d, 2] = jnp.zeros((BLOCK, W), BF)
        for b in range(OWN):
            r = block_rows(b)
            acc2[r] = dot(adj[b], gmg[...], 0, 0)
            before = up[r].astype(F32) if l == LAYERS - 1 else gy[r]
            gy[r] = before + dot(gph[l, r], ws[l], 1, 1)
        if l == 0:
            early.pairs_done(1)
        bundle.core_done()
        bundle.pairs_start(0)
        bundle.pairs_middle(0)
        bundle.pairs_done(0)
        bundle.pairs_start(1)
        if l == 1:
            bundle.pairs_middle(1)
        for c in copies:
            c.wait()

        def message_grad(b, l=l):
            r = block_rows(b)
            total = acc2[r]
            for d in range(4):
                which = jnp.where(sends[0, d] == b, 0, jnp.where(sends[1, d] == b, 1, 2))
                total = total + ret[l][d, which].astype(F32)
            g = (total * pm[l, r]).astype(BF)
            gpm[l, r] = g
            return g

        if l > 0:
            gain_row = jnp.zeros((1, W), F32)
            for b in range(OWN):
                r = block_rows(b)
                g = gy[r] + dot(message_grad(b), wm[l], 1, 1)
                gy[r] = g
                gain_row = gain_row + update_grad(l - 1, b, g, normed[l - 1, r], inverse[l - 1, r])
        else:
            for b in range(OWN):
                message_grad(b)

    weight_grad(tail, 0, xs.at[0], gpm.at[0])
    tail.core_start()
    early.z_start()
    for b in range(OWN):
        r = block_rows(b)
        gy[r] += dot(gpm[0, r], wm[0], 1, 1)
    grad_copy = pltpu.make_async_copy(gy, grad_out, out_sem.at[1])
    grad_copy.start()
    out_copy = pltpu.make_async_copy(xs.at[LAYERS], lat_out, out_sem.at[0])
    out_copy.start()
    tail.core_done()
    tail.plane_start()
    late.pairs_middle(1)
    late.pairs_done(1)
    early.z_done()
    early.gather_start()
    late.z_start()
    tail.plane_done()
    tail.z_start()
    early.gather_done()

    def put(out, l, bundle, tile):
        for q, v in enumerate(bundle.matrix(tile)):
            out[l, :, q * 128 : (q + 1) * 128] = v

    def put_gain(l, bundle, tile):
        v = bundle.matrix(tile)[0]
        same = lax.broadcasted_iota(jnp.int32, v.shape, 0) == lax.broadcasted_iota(jnp.int32, v.shape, 1)
        gg_out[l : l + 1, :] = jnp.sum(jnp.where(same, v, 0.0), axis=0, keepdims=True)[:, :SHARE]

    put(go_out, 1, early, 0)
    put(gs_out, 1, early, 1)
    put(ga_out, 1, early, 2)
    put_gain(1, early, 3)
    late.z_done()
    late.gather_start()
    tail.z_done()
    tail.gather_start()
    late.gather_done()
    put(gm_out, 1, late, 0)
    put(go_out, 0, late, 1)
    put(gs_out, 0, late, 2)
    put(ga_out, 0, late, 3)
    put_gain(0, late, 4)
    tail.gather_done()
    put(gm_out, 0, tail, 0)
    out_copy.wait()
    grad_copy.wait()


PIECES = (2, 4, 1, 1, 1, 1, 1)


def hand_over(*refs):
    count = len(PIECES)
    into, out, held = refs[:count], refs[count : 2 * count], refs[2 * count : 3 * count]
    in_sem, out_sem = refs[3 * count :]
    steps = []
    for i, pieces in enumerate(PIECES):
        size = into[i].shape[0] // pieces
        for j in range(pieces):
            piece = pl.ds(j * size, size)
            n = len(steps)
            steps.append((
                pltpu.make_async_copy(into[i].at[piece], held[i].at[piece], in_sem.at[n]),
                pltpu.make_async_copy(held[i].at[piece], out[i].at[piece], out_sem.at[n]),
            ))
    for first, _ in steps:
        first.start()
    for first, second in steps:
        first.wait()
        second.start()
    for _, second in steps:
        second.wait()


def local(
    latents, upstream, msg_weight, self_weight, agg_weight, out_weight, gains, edge_weight, nbr_slot, send_list
):
    hbm = pl.BlockSpec(memory_space=pl.ANY)
    vmem = pl.BlockSpec(memory_space=pltpu.VMEM)
    share = jax.ShapeDtypeStruct((LAYERS, SHARE, W), F32)
    scratch = [
        pltpu.VMEM((LAYERS + 1, ROWS, W), BF),
        pltpu.VMEM((ROWS, W), BF),
        pltpu.VMEM((LAYERS, W, W), BF),
        pltpu.VMEM((LAYERS, W, W), BF),
        pltpu.VMEM((LAYERS, W, W), BF),
        pltpu.VMEM((LAYERS, W, W), BF),
        pltpu.VMEM((LAYERS, W), F32),
        pltpu.VMEM((OWN, TILES, BLOCK, BLOCK), BF),
        pltpu.SMEM((OWN, TILES), jnp.int32),
        pltpu.SMEM((2, 4), jnp.int32),
        pltpu.VMEM((SLOTS, ROWS, BLOCK), BF),
        pltpu.VMEM((LAYERS, OWN, BLOCK, W), BF),
        pltpu.VMEM((LAYERS, 4, 2, BLOCK, W), BF),
        pltpu.VMEM((LAYERS, 4, 2, BLOCK, W), BF),
        pltpu.VMEM((LAYERS, 4, 2, BLOCK, W), BF),
        pltpu.VMEM((4, 3, BLOCK, W), BF),
        pltpu.VMEM((4, 3, BLOCK, W), BF),
        pltpu.VMEM((LAYERS, ROWS, W), F32),
        pltpu.VMEM((LAYERS, ROWS, W), F32),
        pltpu.VMEM((LAYERS, ROWS, W), F32),
        pltpu.VMEM((LAYERS, ROWS, 1), F32),
        pltpu.VMEM((LAYERS, ROWS, W), BF),
        pltpu.VMEM((LAYERS, ROWS, W), BF),
        pltpu.VMEM((ROWS, W), F32),
        pltpu.VMEM((ROWS, W), F32),
        pltpu.VMEM((ROWS, W), F32),
        pltpu.VMEM((LAYERS, ROWS, W), BF),
        pltpu.VMEM((LAYERS, ROWS, W), BF),
        pltpu.VMEM((ROWS, W), BF),
        pltpu.VMEM((LAYERS, ROWS, W), BF),
        pltpu.SemaphoreType.DMA((10,)),
        pltpu.SemaphoreType.DMA((2,)),
        pltpu.SemaphoreType.DMA((2 * LAYERS, 4)),
        pltpu.SemaphoreType.DMA((2 * LAYERS, 4)),
    ]
    for i, tiles in enumerate(BUNDLE_TILES):
        scratch += bundle_scratch(tiles, i == 2)
    shapes = (
        jax.ShapeDtypeStruct((ROWS, W), BF),
        jax.ShapeDtypeStruct((ROWS, W), F32),
        share, share, share, share,
        jax.ShapeDtypeStruct((LAYERS, SHARE), F32),
    )
    out = pl.pallas_call(
        kernel,
        out_shape=shapes,
        in_specs=[hbm] * 10,
        out_specs=(hbm, hbm, vmem, vmem, vmem, vmem, vmem),
        scratch_shapes=scratch,
        compiler_params=pltpu.CompilerParams(
            collective_id=0, has_side_effects=True, vmem_limit_bytes=60 * 1024 * 1024
        ),
        cost_estimate=pl.CostEstimate(flops=10 * 10**9, bytes_accessed=10 * 2**20, transcendentals=2 * 10**6),
    )(latents, upstream, msg_weight, self_weight, agg_weight, out_weight, gains, edge_weight, nbr_slot, jnp.swapaxes(send_list, 2, 3))
    return pl.pallas_call(
        hand_over,
        out_shape=shapes,
        in_specs=[hbm] * 7,
        out_specs=[hbm] * 7,
        scratch_shapes=[pltpu.VMEM(v.shape, v.dtype) for v in shapes]
        + [pltpu.SemaphoreType.DMA((sum(PIECES),)), pltpu.SemaphoreType.DMA((sum(PIECES),))],
    )(*out)


def solution(mesh):
    rows = P(("space", "slab"), None)
    return jax.shard_map(
        local,
        mesh=mesh,
        in_specs=(
            rows, rows, P(), P(), P(), P(), P(),
            P(("space", "slab"), None, None, None), rows, P("space", "slab", None, None),
        ),
        out_specs=(
            rows, rows, P(None, "space", None), P(None, "space", None), P(None, "space", None),
            P(None, "space", None), P(None, "space"),
        ),
        check_vma=False,
    )
```

time: 146 us -> 121 us (0.83)
  Pallas kernels: 136 us -> 120 us
  local copies, waits for them, and re-layouts: 8.09 us -> 0 us
    pallas_call x1 -> x2, Pallas kernels: 136 us -> 120 us  [the longest x1 117 us: local(): pl.pallas_call(kernel, out_shape=shapes, in_specs=[hbm] * 10, out_specs=(...]
    unnamed x21 -> x0, local copies, waits for them, and re-layouts: 7.43 us -> none
where the time goes in v2:
time: 121 us
  Pallas kernels  120 us (99%)
    pallas_call x1, Pallas kernels, local(): pl.pallas_call(kernel, out_shape=shapes, in_specs=[hbm] * 10, out_specs=(...  117 us

profile of v2, /device:TPU:8, one launch (start us, length us, event | category | flops | bytes accessed | tf_op | source)
XLA Modules:
  0.0 120.6 jit_solution(18281419351707556429)
XLA Ops:
  0.6 117.4 %shard_map.153 = (bf16[512,512]{1,0:T(8,128)(2,1)}, f32[512,512]{1,0:T(8,128)}, f32[2,16,512]{2,1,0:T(8,128)}, f32[2,16,512]{2,1,0:T(8,128)}, f32[2,16,512]{2,1,...) custom-call(bf16[512,512]{1,0:T(8,128)(2,1)} %lat_in.1, bf16[512,512]{1,0:T(8,128)(2,1)} %up_in.1, ...), custom_call_target="tpu_custom_call" | custom-call | flops 10000000000 | bytes 10485760 | tf_op jit(solution)/shard_map/pallas_call | solution.py:571
  118.1 2.4 %shard_map.154 = (bf16[512,512]{1,0:T(8,128)(2,1)}, f32[512,512]{1,0:T(8,128)}, f32[2,16,512]{2,1,0:T(8,128)}, f32[2,16,512]{2,1,0:T(8,128)}, f32[2,16,512]{2,1,...) custom-call(bf16[512,512]{1,0:T(8,128)(2,1)} %get-tuple-element.14.refs_0_, f32[512,512]{1,0:T(8,128)} %get-tuple-element.15.refs_1_, ...), custom_call_target="tpu_custom_call" | custom-call | tf_op jit(solution)/shard_map/pallas_call | solution.py:582

commit v3 on v2

v3 whole, which is shorter than its diff:
```python
import jax
import jax.numpy as jnp
from jax import lax
from jax.experimental import pallas as pl
from jax.experimental.pallas import tpu as pltpu
from jax.sharding import PartitionSpec as P

EPS = 1e-05
BF = jnp.bfloat16
F32 = jnp.float32
MESH = pl.DeviceIdType.MESH

W = 512
BLOCK = 128
OWN = 4
TILES = 6
SLOTS = 12
ROWS = OWN * BLOCK
COLS = SLOTS * BLOCK
LAYERS = 2
NY, NZH, NCORE = 4, 4, 2
NX, NZL = 4, 2
NZ = NZH * NZL
N_SPACE = NY * NZH * NCORE
N_SLAB = NX * NZL
SHARE = W // N_SPACE

BUNDLE_TILES = (2, 2)
ORDER = (2, 3, 0, 1)
ORDER_IN = (0, 1, 2, 3)
HALF = NZH // 2
HALO_ROWS = 2 * BLOCK


def sigmoid(v):
    return 0.5 * jnp.tanh(0.5 * v) + 0.5


def slope(v, s):
    return s * (1.0 + v * (1.0 - s))


def dot(a, b, ca, cb):
    return lax.dot_general(a, b, (((ca,), (cb,)), ((), ())), preferred_element_type=F32)


def loop(count, body):
    def step(i, carry):
        body(i)
        return carry

    lax.fori_loop(0, count, step, 0)


def rows_of(i, size):
    return pl.ds(pl.multiple_of(i * size, size), size)


def block_rows(b):
    return slice(b * BLOCK, (b + 1) * BLOCK)


def add(dst, *others):
    total = dst[...].astype(F32)
    for other in others:
        total = total + other[...].astype(F32)
    dst[...] = total.astype(BF)


class Bundle:
    def __init__(self, refs, place):
        self.grad, self.held, self.z, self.full, self.send, self.recv, *self.land = refs
        self.place = place
        self.next = 0

    def copy(self, src, dst, device):
        i = self.next
        self.next += 1
        c = pltpu.make_async_remote_copy(
            src_ref=src, dst_ref=dst, send_sem=self.send.at[i], recv_sem=self.recv.at[i],
            device_id=device, device_id_type=MESH,
        )
        c.start()
        return c

    def core_start(self):
        core = self.place["core"]
        self.core_copy = self.copy(self.grad.at[1 - core], self.held, self.place["at"](core=1 - core))

    def core_done(self):
        core = self.place["core"]
        self.core_copy.wait()

        def body(i):
            self.held[i] = (self.held[i].astype(F32) + self.grad[core, i].astype(F32)).astype(BF)

        loop(NY, body)

    def z_start(self):
        place = self.place
        z = place["zh"] * NZL + place["zl"]
        self.z_copies = []
        for j in range(1, NZ):
            there = lax.rem(z + j, NZ)
            zh, zl = there // NZL, lax.rem(there, NZL)
            self.z_copies.append(
                self.copy(self.held.at[place["y"], place["x"], zh], self.z.at[j - 1], place["at"](zh=zh, zl=zl))
            )

    def z_done(self):
        place = self.place
        total = self.held[place["y"], place["x"], place["zh"]].astype(F32)
        for j, c in enumerate(self.z_copies):
            c.wait()
            total = total + self.z[j].astype(F32)
        self.full[place["x"]] = total.astype(BF)

    def gather_start(self):
        place = self.place
        mine = self.full.at[place["x"]]
        self.gather_copies = [
            self.copy(mine, mine, place["at"](x=lax.rem(place["x"] + j, NX))) for j in range(1, NX)
        ]

    def gather_done(self):
        for c in self.gather_copies:
            c.wait()

    def matrix(self, tile):
        return [self.full[q, :, tile * 128 : (tile + 1) * 128].astype(F32) for q in range(NX)]


    def cross(self, stage, half, axis, i):
        part = pl.ds(half * HALF, HALF)
        y, x = self.place["y"], self.place["x"]
        if stage == 0:
            return self.held.at[i, :, part] if axis == "y" else self.held.at[:, i, part]
        return self.held.at[i, x, part] if axis == "y" else self.held.at[y, i, part]

    def plane_start(self, stage):
        place = self.place
        self.plane = []
        for half, axis in enumerate(("y", "x") if stage == 0 else ("x", "y")):
            for j in range(1, 4):
                there = lax.rem(place[axis] + j, 4)
                self.plane.append(
                    self.copy(self.cross(stage, half, axis, there), self.land[stage].at[half, j - 1],
                              place["at"](**{axis: there}))
                )

    def plane_done(self, stage):
        place = self.place
        for c in self.plane:
            c.wait()
        for half, axis in enumerate(("y", "x") if stage == 0 else ("x", "y")):
            add(self.cross(stage, half, axis, place[axis]), *[self.land[stage].at[half, j] for j in range(3)])


class Gains:
    def __init__(self, refs, place):
        self.sums, self.land, self.send, self.recv = refs
        self.place = place

    def start(self, stage):
        place = self.place
        first = (0, 1, 4, 7)[stage]
        peers = []
        if stage == 0:
            peers = [place["at"](core=1 - place["core"])]
        elif stage < 3:
            axis = "yx"[stage - 1]
            peers = [place["at"](**{axis: lax.rem(place[axis] + j, 4)}) for j in range(1, 4)]
        else:
            z = place["zh"] * NZL + place["zl"]
            for j in range(1, NZ):
                there = lax.rem(z + j, NZ)
                peers.append(place["at"](zh=there // NZL, zl=lax.rem(there, NZL)))
        self.copies = []
        for i, peer in enumerate(peers):
            c = pltpu.make_async_remote_copy(
                src_ref=self.sums.at[stage], dst_ref=self.land.at[first + i], send_sem=self.send.at[first + i],
                recv_sem=self.recv.at[first + i], device_id=peer, device_id_type=MESH,
            )
            c.start()
            self.copies.append(c)

    def done(self, stage):
        first = (0, 1, 4, 7)[stage]
        total = self.sums[stage]
        for i, c in enumerate(self.copies):
            c.wait()
            total = total + self.land[first + i]
        self.sums[stage + 1] = total


def bundle_scratch(tiles):
    c = tiles * 128
    copies = 1 + 6 + 6 + (NZ - 1) + (NX - 1)
    return [
        pltpu.VMEM((NCORE, NY, NX, NZH, SHARE, c), BF),
        pltpu.VMEM((NY, NX, NZH, SHARE, c), BF),
        pltpu.VMEM((NZ - 1, SHARE, c), BF),
        pltpu.VMEM((NX, SHARE, c), BF),
        pltpu.SemaphoreType.DMA((copies,)),
        pltpu.SemaphoreType.DMA((copies,)),
        pltpu.VMEM((2, 3, 4, HALF, SHARE, c), BF),
        pltpu.VMEM((2, 3, HALF, SHARE, c), BF),
    ]


def kernel(
    lat_in, up_in, wm_in, ws_in, wa_in, wo_in, gains_in, edge_in, nbr_in, sends_in,
    lat_out, grad_out, gm_out, gs_out, ga_out, go_out, gg_out,
    xs, up, wm, ws, wa, wo, gains, edge, nbr, sends, adj, own, xh, mh, out_blocks, back, ret0, ret1,
    pm, pmh, ph, normed, inverse, merged, hidden, acc, acc2, gy, gu, gph, gmg, gpm, gpmh, in_sem, out_sem,
    halo_send, halo_recv, gain_sums, gain_land, gain_send, gain_recv, *bundle_refs,
):
    space = lax.axis_index("space")
    slab = lax.axis_index("slab")
    core = lax.rem(space, NCORE)
    zh = lax.rem(space // NCORE, NZH)
    y = space // (NCORE * NZH)
    zl = lax.rem(slab, NZL)
    x = slab // NZL

    def at(**new):
        p = {"core": core, "zh": zh, "y": y, "zl": zl, "x": x, **new}
        return ((p["y"] * NZH + p["zh"]) * NCORE + p["core"], p["x"] * NZL + p["zl"])

    place = {"core": core, "zh": zh, "y": y, "zl": zl, "x": x, "at": at}
    s_up, s_down = lax.rem(space + 1, N_SPACE), lax.rem(space + N_SPACE - 1, N_SPACE)
    l_up, l_down = lax.rem(slab + 1, N_SLAB), lax.rem(slab + N_SLAB - 1, N_SLAB)
    ahead = [(s_up, slab), (s_down, slab), (space, l_up), (space, l_down)]
    behind = [ahead[1], ahead[0], ahead[3], ahead[2]]

    barrier = pltpu.get_barrier_semaphore()
    partners = list(ahead) + [at(core=1 - core)]
    partners += [at(y=lax.rem(y + i, NY), x=lax.rem(x + j, NX)) for i in range(NY) for j in range(NX) if i or j]
    z = zh * NZL + zl
    for j in range(1, NZ):
        there = lax.rem(z + j, NZ)
        partners.append(at(zh=there // NZL, zl=lax.rem(there, NZL)))
    for p in partners:
        pl.semaphore_signal(barrier, inc=1, device_id=p, device_id_type=MESH)

    pairs = [
        (lat_in, xs.at[0]), (sends_in.at[0, 0], sends), (wm_in, wm), (nbr_in, nbr), (edge_in, edge), (ws_in, ws),
        (wa_in, wa), (wo_in, wo), (gains_in, gains), (up_in, up),
    ]
    loads = [pltpu.make_async_copy(a, b, in_sem.at[i]) for i, (a, b) in enumerate(pairs)]
    for c in loads:
        c.start()
    lat_load, sends_load, wm_load, nbr_load, edge_load, ws_load, wa_load, wo_load, gains_load, up_load = loads

    count = len(bundle_scratch(1))
    bundles = [Bundle(bundle_refs[i * count : (i + 1) * count], place) for i in range(2 * LAYERS)]
    ret = (ret0, ret1)
    gain = Gains((gain_sums, gain_land, gain_send, gain_recv), place)

    def halo(src, dst, peers, exchange, before):
        copies = {}
        for d in ORDER:
            before(d)
            copies[d] = pltpu.make_async_remote_copy(
                src_ref=src(d), dst_ref=dst(d), send_sem=halo_send.at[exchange, d],
                recv_sem=halo_recv.at[exchange, d], device_id=peers[d], device_id_type=MESH,
            )
            copies[d].start()
        return copies

    def adjacency(e, blocks, rows=slice(None)):
        return jnp.concatenate([adj[e + j, rows] for j in range(blocks)], axis=1)

    def halo_rows(d):
        return slice(d * HALO_ROWS, (d + 1) * HALO_ROWS)

    def picked(l):
        def pick(d):
            for t in range(2):
                out_blocks[l, d, block_rows(t)] = xs[l, sends[t, d]]

        return pick

    lat_load.wait()
    sends_load.wait()
    pl.semaphore_wait(barrier, len(partners))
    wide = [slice(i * 256, (i + 1) * 256) for i in range(ROWS // 256)]

    def update_grad(l, cotangent):
        row = jnp.zeros((1, W), F32)
        for r in wide:
            g = cotangent(r)
            n = normed[l, r]
            row = row + jnp.sum(g * n, axis=0, keepdims=True)
            g = g * gains[l : l + 1, :]
            u = g - jnp.mean(g, axis=-1, keepdims=True) - n * jnp.mean(g * n, axis=-1, keepdims=True)
            gu[l, r] = (inverse[l, r] * u).astype(BF)
        for r in wide:
            gph[l, r] = (dot(gu[l, r], wo[l], 1, 1) * ph[l, r]).astype(BF)
        for r in wide:
            gmg[r] = dot(gph[l, r], wa[l], 1, 1).astype(BF)
        gain_sums[0, l : l + 1, :] = row

    for l in range(LAYERS):
        copies = halo(
            lambda d: out_blocks.at[l, d], lambda d: xh.at[l, pl.ds(d * HALO_ROWS, HALO_ROWS)], ahead, l, picked(l)
        )
        if l == 0:
            wm_load.wait()
        for b in range(OWN):
            r = block_rows(b)
            v = dot(xs[l, b], wm[l], 1, 0)
            s = sigmoid(v)
            own[r] = (v * s).astype(BF)
            pm[l, r] = slope(v, s)
        if l == 0:
            edge_load.wait()
            nbr_load.wait()

            def build(i):
                b = i // SLOTS
                e = lax.rem(i, SLOTS)
                total = jnp.zeros((BLOCK, BLOCK), F32)
                for k in range(TILES):
                    keep = jnp.where(nbr[b, k] == e, 1.0, 0.0)
                    total = total + edge[b, k].astype(F32) * keep
                adj[e, rows_of(b, BLOCK), :] = total.astype(BF)

            loop(OWN * SLOTS, build)
            for c in (ws_load, wa_load, wo_load, gains_load, up_load):
                c.wait()
        for b in range(OWN):
            r = block_rows(b)
            ph[l, r] = dot(xs[l, b], ws[l], 1, 0)
            acc[r] = dot(adjacency(0, OWN, r), own[...], 1, 0)
        if l > 0:
            for i in range(4 * HALO_ROWS // BLOCK):
                r = block_rows(i)
                v = pmh[l - 1, r]
                pmh[l - 1, r] = slope(v, sigmoid(v))
        for d in ORDER_IN:
            copies[d].wait()
            for t in range(2):
                r = slice(d * HALO_ROWS + t * BLOCK, d * HALO_ROWS + (t + 1) * BLOCK)
                v = dot(xh[l, r], wm[l], 1, 0)
                pmh[l, r] = v
                mh[r] = (v * sigmoid(v)).astype(BF)
            if d != ORDER_IN[-1]:
                for b in range(OWN):
                    r = block_rows(b)
                    acc[r] += dot(adjacency(OWN + 2 * d, 2, r), mh[halo_rows(d)], 1, 0)
        d = ORDER_IN[-1]
        last = mh[halo_rows(d)]
        for b in range(OWN):
            r = block_rows(b)
            merged[l, r] = (acc[r] + dot(adjacency(OWN + 2 * d, 2, r), last, 1, 0)).astype(BF)
        for b in range(OWN):
            r = block_rows(b)
            v = ph[l, r] + dot(merged[l, r], wa[l], 1, 0)
            s = sigmoid(v)
            hidden[l, r] = (v * s).astype(BF)
            ph[l, r] = slope(v, s)
        updates = [dot(hidden[l, block_rows(b)], wo[l], 1, 0) for b in range(OWN)]
        for b, u in enumerate(updates):
            r = block_rows(b)
            centred = u - jnp.mean(u, axis=-1, keepdims=True)
            inv = lax.rsqrt(jnp.mean(centred * centred, axis=-1, keepdims=True) + EPS)
            n = centred * inv
            xs[l + 1, b] = (xs[l, b].astype(F32) + gains[l : l + 1, :] * n).astype(BF)
            normed[l, r] = n
            inverse[l, r] = inv

    update_grad(LAYERS - 1, lambda r: up[r].astype(F32))
    out_copy = pltpu.make_async_copy(xs.at[LAYERS], lat_out, out_sem.at[0])
    out_copy.start()

    def weight_grad(bundle, tile, *pairs):
        for i in range(2):
            r = pl.ds(i * 256, 256)
            v = sum(dot(a(r), g[...], 0, 0) for a, g in pairs)
            v = v.astype(BF).reshape(2, NZH, NCORE, SHARE, W)
            for c in range(NCORE):
                for q in range(NX):
                    bundle.grad[c, pl.ds(2 * i, 2), q, :, :, tile * 128 : (tile + 1) * 128] = v[
                        :, :, c, :, q * 128 : (q + 1) * 128
                    ]

    def put(out, l, bundle, tile):
        for q, v in enumerate(bundle.matrix(tile)):
            out[l, :, q * 128 : (q + 1) * 128] = v

    def put_gains():
        pick = lax.broadcasted_iota(jnp.int32, (W, SHARE), 0) - space * SHARE
        pick = (pick == lax.broadcasted_iota(jnp.int32, (W, SHARE), 1)).astype(F32)
        gg_out[...] = lax.dot_general(
            gain_sums[4], pick, (((1,), (0,)), ((), ())), precision=lax.Precision.HIGHEST, preferred_element_type=F32
        )

    def put_all(l, one, two):
        one.gather_done()
        put(go_out, l, one, 0)
        put(gs_out, l, one, 1)
        two.gather_done()
        put(ga_out, l, two, 0)
        put(gm_out, l, two, 1)

    def z_to_gather(one, two):
        for bundle in (one, two):
            bundle.z_done()
            bundle.gather_start()

    earlier = None
    for l in reversed(range(LAYERS)):

        def back_grad(d, l=l):
            v = dot(adjacency(OWN + 2 * d, 2), gmg[...], 0, 0)
            back[l, d] = v.astype(BF).reshape(2, BLOCK, W)

        copies = halo(
            lambda d: back.at[l, d], lambda d: ret[l].at[d, pl.ds(0, 2)], behind, LAYERS + l, back_grad
        )

        one, two = bundles[2 * l], bundles[2 * l + 1]
        if earlier:
            gain.start(0)
            for bundle in earlier:
                bundle.plane_done(0)
                bundle.plane_start(1)

        def latent_columns(r, l=l):
            return xs[l, :, :, r].reshape(ROWS, 256)

        weight_grad(one, 0, (lambda r: hidden[l, :, r], gu.at[l]))
        weight_grad(one, 1, (latent_columns, gph.at[l]))
        one.core_start()
        for b in range(OWN):
            r = block_rows(b)
            v = dot(adj[b], gmg[...], 0, 0)
            acc2[r] = v
            gpm[r] = (v * pm[l, r]).astype(BF)
        for i in range(4 * HALO_ROWS // BLOCK):
            r = block_rows(i)
            v = pmh[l, r]
            if l == LAYERS - 1:
                v = slope(v, sigmoid(v))
            gpmh[r] = (back[l, i // 2, i % 2].astype(F32) * v).astype(BF)
        weight_grad(two, 0, (lambda r: merged[l, :, r], gph.at[l]))
        weight_grad(two, 1, (latent_columns, gpm), (lambda r: xh[l, :, r], gpmh))
        two.core_start()
        if earlier:
            for bundle in earlier:
                bundle.plane_done(1)
                bundle.z_start()
            gain.done(0)
            gain.start(1)
        for d in range(4):
            ret[l][d, 2] = jnp.zeros((BLOCK, W), BF)
        one.core_done()
        one.plane_start(0)
        for b in range(OWN):
            r = block_rows(b)
            before = up[r].astype(F32) if l == LAYERS - 1 else gy[r]
            gy[r] = before + dot(gph[l, r], ws[l], 1, 1)
        two.core_done()
        two.plane_start(0)
        if earlier:
            gain.done(1)
            gain.start(2)
            z_to_gather(*earlier)
            for bundle in (one, two):
                bundle.plane_done(0)
                bundle.plane_start(1)
            gain.done(2)
            gain.start(3)
            put_all(l + 1, *earlier)
            for bundle in (one, two):
                bundle.plane_done(1)
                bundle.z_start()
        for d in ORDER:
            copies[d].wait()

        def message_grad(b, l=l):
            r = block_rows(b)
            total = acc2[r]
            for d in range(4):
                which = jnp.where(sends[0, d] == b, 0, jnp.where(sends[1, d] == b, 1, 2))
                total = total + ret[l][d, which].astype(F32)
            gpm[r] = (total * pm[l, r]).astype(BF)

        for b in range(OWN):
            message_grad(b)
        for r in wide:
            gy[r] += dot(gpm[r], wm[l], 1, 1)
        if l > 0:
            update_grad(l - 1, lambda r: gy[r])
        earlier = (one, two)

    grad_copy = pltpu.make_async_copy(gy, grad_out, out_sem.at[1])
    grad_copy.start()
    z_to_gather(*earlier)
    gain.done(3)
    put_gains()
    put_all(0, *earlier)
    out_copy.wait()
    grad_copy.wait()


PIECES = (2, 4, 1, 1, 1, 1, 1)


def hand_over(*refs):
    count = len(PIECES)
    into, out, held = refs[:count], refs[count : 2 * count], refs[2 * count : 3 * count]
    in_sem, out_sem = refs[3 * count :]
    steps = []
    for i, pieces in enumerate(PIECES):
        size = into[i].shape[0] // pieces
        for j in range(pieces):
            piece = pl.ds(j * size, size)
            n = len(steps)
            steps.append((
                pltpu.make_async_copy(into[i].at[piece], held[i].at[piece], in_sem.at[n]),
                pltpu.make_async_copy(held[i].at[piece], out[i].at[piece], out_sem.at[n]),
            ))
    for first, _ in steps:
        first.start()
    for first, second in steps:
        first.wait()
        second.start()
    for _, second in steps:
        second.wait()


def local(
    latents, upstream, msg_weight, self_weight, agg_weight, out_weight, gains, edge_weight, nbr_slot, send_list
):
    hbm = pl.BlockSpec(memory_space=pl.ANY)
    vmem = pl.BlockSpec(memory_space=pltpu.VMEM)
    share = jax.ShapeDtypeStruct((LAYERS, SHARE, W), F32)
    scratch = [
        pltpu.VMEM((LAYERS + 1, OWN, BLOCK, W), BF),
        pltpu.VMEM((ROWS, W), BF),
        pltpu.VMEM((LAYERS, W, W), BF),
        pltpu.VMEM((LAYERS, W, W), BF),
        pltpu.VMEM((LAYERS, W, W), BF),
        pltpu.VMEM((LAYERS, W, W), BF),
        pltpu.VMEM((LAYERS, W), F32),
        pltpu.VMEM((OWN, TILES, BLOCK, BLOCK), BF),
        pltpu.SMEM((OWN, TILES), jnp.int32),
        pltpu.SMEM((2, 4), jnp.int32),
        pltpu.VMEM((SLOTS, ROWS, BLOCK), BF),
        pltpu.VMEM((ROWS, W), BF),
        pltpu.VMEM((LAYERS, 4 * HALO_ROWS, W), BF),
        pltpu.VMEM((4 * HALO_ROWS, W), BF),
        pltpu.VMEM((LAYERS, 4, HALO_ROWS, W), BF),
        pltpu.VMEM((LAYERS, 4, 2, BLOCK, W), BF),
        pltpu.VMEM((4, 3, BLOCK, W), BF),
        pltpu.VMEM((4, 3, BLOCK, W), BF),
        pltpu.VMEM((LAYERS, ROWS, W), F32),
        pltpu.VMEM((LAYERS, 4 * HALO_ROWS, W), F32),
        pltpu.VMEM((LAYERS, ROWS, W), F32),
        pltpu.VMEM((LAYERS, ROWS, W), F32),
        pltpu.VMEM((LAYERS, ROWS, 1), F32),
        pltpu.VMEM((LAYERS, ROWS, W), BF),
        pltpu.VMEM((LAYERS, ROWS, W), BF),
        pltpu.VMEM((ROWS, W), F32),
        pltpu.VMEM((ROWS, W), F32),
        pltpu.VMEM((ROWS, W), F32),
        pltpu.VMEM((LAYERS, ROWS, W), BF),
        pltpu.VMEM((LAYERS, ROWS, W), BF),
        pltpu.VMEM((ROWS, W), BF),
        pltpu.VMEM((ROWS, W), BF),
        pltpu.VMEM((4 * HALO_ROWS, W), BF),
        pltpu.SemaphoreType.DMA((10,)),
        pltpu.SemaphoreType.DMA((2,)),
        pltpu.SemaphoreType.DMA((2 * LAYERS, 4)),
        pltpu.SemaphoreType.DMA((2 * LAYERS, 4)),
        pltpu.VMEM((5, LAYERS, W), F32),
        pltpu.VMEM((14, LAYERS, W), F32),
        pltpu.SemaphoreType.DMA((14,)),
        pltpu.SemaphoreType.DMA((14,)),
    ]
    for tiles in BUNDLE_TILES * LAYERS:
        scratch += bundle_scratch(tiles)
    shapes = (
        jax.ShapeDtypeStruct((OWN, BLOCK, W), BF),
        jax.ShapeDtypeStruct((ROWS, W), F32),
        share, share, share, share,
        jax.ShapeDtypeStruct((LAYERS, SHARE), F32),
    )
    out = pl.pallas_call(
        kernel,
        out_shape=shapes,
        in_specs=[hbm] * 10,
        out_specs=(hbm, hbm, vmem, vmem, vmem, vmem, vmem),
        scratch_shapes=scratch,
        compiler_params=pltpu.CompilerParams(
            collective_id=0, has_side_effects=True, vmem_limit_bytes=60 * 1024 * 1024
        ),
        cost_estimate=pl.CostEstimate(flops=10 * 10**9, bytes_accessed=10 * 2**20, transcendentals=2 * 10**6),
    )(latents.reshape(OWN, BLOCK, W), upstream, msg_weight, self_weight, agg_weight, out_weight, gains, edge_weight, nbr_slot, jnp.swapaxes(send_list, 2, 3))
    first, *rest = pl.pallas_call(
        hand_over,
        out_shape=shapes,
        in_specs=[hbm] * 7,
        out_specs=[hbm] * 7,
        scratch_shapes=[pltpu.VMEM(v.shape, v.dtype) for v in shapes]
        + [pltpu.SemaphoreType.DMA((sum(PIECES),)), pltpu.SemaphoreType.DMA((sum(PIECES),))],
    )(*out)
    return (first.reshape(ROWS, W), *rest)


def solution(mesh):
    rows = P(("space", "slab"), None)
    return jax.shard_map(
        local,
        mesh=mesh,
        in_specs=(
            rows, rows, P(), P(), P(), P(), P(),
            P(("space", "slab"), None, None, None), rows, P("space", "slab", None, None),
        ),
        out_specs=(
            rows, rows, P(None, "space", None), P(None, "space", None), P(None, "space", None),
            P(None, "space", None), P(None, "space"),
        ),
        check_vma=False,
    )
```

time: 121 us -> 114 us (0.942)
  Pallas kernels: 120 us -> 113 us
    pallas_call x1, Pallas kernels: 117 us -> 110 us  [local(): pl.pallas_call(kernel, out_shape=shapes, in_specs=[hbm] * 10, out_specs=(...]
where the time goes in v3:
time: 114 us; the launch traced here: 113 us
  Pallas kernels  113 us (99%)
    pallas_call x1, Pallas kernels, local(): pl.pallas_call(kernel, out_shape=shapes, in_specs=[hbm] * 10, out_specs=(...  110 us
    pallas_call x1, Pallas kernels, local(): pl.pallas_call(hand_over, out_shape=shapes, in_specs=[hbm] * 7, out_specs...  2.36 us

profile of v3, /device:TPU:8, one launch (start us, length us, event | category | flops | bytes accessed | tf_op | source)
XLA Modules:
  0.0 113.3 jit_solution(15947348157561458237)
XLA Ops:
  0.6 110.2 %shard_map.153 = (bf16[4,128,512]{2,1,0:T(8,128)(2,1)}, f32[512,512]{1,0:T(8,128)}, f32[2,16,512]{2,1,0:T(8,128)}, f32[2,16,512]{2,1,0:T(8,128)}, f32[2,16,512]{...) custom-call(bf16[4,128,512]{2,1,0:T(8,128)(2,1)} %bitcast.3, bf16[512,512]{1,0:T(8,128)(2,1)} %up_in.1, ...), custom_call_target="tpu_custom_call" | custom-call | flops 10000000000 | bytes 10485760 | tf_op jit(solution)/shard_map/pallas_call | solution.py:591
  110.8 2.4 %shard_map.154 = (bf16[4,128,512]{2,1,0:T(8,128)(2,1)}, f32[512,512]{1,0:T(8,128)}, f32[2,16,512]{2,1,0:T(8,128)}, f32[2,16,512]{2,1,0:T(8,128)}, f32[2,16,512]{...) custom-call(bf16[4,128,512]{2,1,0:T(8,128)(2,1)} %get-tuple-element.21.refs_0_, ...), custom_call_target="tpu_custom_call" | custom-call | tf_op jit(solution)/shard_map/pallas_call | solution.py:602

commit v4 on v3

--- a/solution.py
+++ b/solution.py
@@ -26,9 +26,9 @@
 SHARE = W // N_SPACE
 
 BUNDLE_TILES = (2, 2)
-ORDER = (2, 3, 0, 1)
+ORDER = (0, 1, 2, 3)
 ORDER_IN = (0, 1, 2, 3)
-HALF = NZH // 2
+Y_FIRST = (3, 3)
 HALO_ROWS = 2 * BLOCK
 
 
@@ -68,7 +68,8 @@
 
 
 class Bundle:
-    def __init__(self, refs, place):
+    def __init__(self, refs, place, y_first):
+        self.y_first = y_first
         self.grad, self.held, self.z, self.full, self.send, self.recv, *self.land = refs
         self.place = place
         self.next = 0
@@ -104,56 +105,69 @@
             there = lax.rem(z + j, NZ)
             zh, zl = there // NZL, lax.rem(there, NZL)
             self.z_copies.append(
-                self.copy(self.held.at[place["y"], place["x"], zh], self.z.at[j - 1], place["at"](zh=zh, zl=zl))
+                self.copy(self.held.at[place["y"], place["x"], zh, :, rows_of(zl, 128)], self.z.at[j - 1],
+                          place["at"](zh=zh, zl=zl))
             )
 
     def z_done(self):
         place = self.place
-        total = self.held[place["y"], place["x"], place["zh"]].astype(F32)
+        total = self.held[place["y"], place["x"], place["zh"], :, rows_of(place["zl"], 128)].astype(F32)
         for j, c in enumerate(self.z_copies):
             c.wait()
             total = total + self.z[j].astype(F32)
-        self.full[place["x"]] = total.astype(BF)
+        self.full[place["x"], place["zl"]] = total.astype(BF)
 
     def gather_start(self):
         place = self.place
-        mine = self.full.at[place["x"]]
-        self.gather_copies = [
-            self.copy(mine, mine, place["at"](x=lax.rem(place["x"] + j, NX))) for j in range(1, NX)
-        ]
+        mine = self.full.at[place["x"], place["zl"]]
+        slab = place["x"] * NZL + place["zl"]
+        self.gather_copies = []
+        for j in range(1, N_SLAB):
+            there = lax.rem(slab + j, N_SLAB)
+            self.gather_copies.append(self.copy(mine, mine, place["at"](x=there // NZL, zl=lax.rem(there, NZL))))
 
     def gather_done(self):
         for c in self.gather_copies:
             c.wait()
 
     def matrix(self, tile):
-        return [self.full[q, :, tile * 128 : (tile + 1) * 128].astype(F32) for q in range(NX)]
-
-
-    def cross(self, stage, half, axis, i):
-        part = pl.ds(half * HALF, HALF)
+        return [self.full[q, tile].astype(F32) for q in range(NX)]
+
+
+    def ways(self, stage):
+        cut = self.y_first
+        ways = [("yx"[stage], pl.ds(0, cut))]
+        if cut < NZH:
+            ways.append(("xy"[stage], pl.ds(cut, NZH - cut)))
+        return ways
+
+    def cross(self, stage, part, axis, i):
         y, x = self.place["y"], self.place["x"]
         if stage == 0:
             return self.held.at[i, :, part] if axis == "y" else self.held.at[:, i, part]
         return self.held.at[i, x, part] if axis == "y" else self.held.at[y, i, part]
 
+    def landing(self, stage, part, j):
+        if stage == 0:
+            return self.land[0].at[j, :, part]
+        return self.land[1].at[j, part]
+
     def plane_start(self, stage):
         place = self.place
         self.plane = []
-        for half, axis in enumerate(("y", "x") if stage == 0 else ("x", "y")):
+        for axis, part in self.ways(stage):
             for j in range(1, 4):
                 there = lax.rem(place[axis] + j, 4)
                 self.plane.append(
-                    self.copy(self.cross(stage, half, axis, there), self.land[stage].at[half, j - 1],
+                    self.copy(self.cross(stage, part, axis, there), self.landing(stage, part, j - 1),
                               place["at"](**{axis: there}))
                 )
 
     def plane_done(self, stage):
-        place = self.place
         for c in self.plane:
             c.wait()
-        for half, axis in enumerate(("y", "x") if stage == 0 else ("x", "y")):
-            add(self.cross(stage, half, axis, place[axis]), *[self.land[stage].at[half, j] for j in range(3)])
+        for axis, part in self.ways(stage):
+            add(self.cross(stage, part, axis, self.place[axis]), *[self.landing(stage, part, j) for j in range(3)])
 
 
 class Gains:
@@ -195,16 +209,16 @@
 
 def bundle_scratch(tiles):
     c = tiles * 128
-    copies = 1 + 6 + 6 + (NZ - 1) + (NX - 1)
+    copies = 1 + 6 + 6 + (NZ - 1) + (N_SLAB - 1)
     return [
         pltpu.VMEM((NCORE, NY, NX, NZH, SHARE, c), BF),
         pltpu.VMEM((NY, NX, NZH, SHARE, c), BF),
-        pltpu.VMEM((NZ - 1, SHARE, c), BF),
-        pltpu.VMEM((NX, SHARE, c), BF),
+        pltpu.VMEM((NZ - 1, SHARE, 128), BF),
+        pltpu.VMEM((NX, NZL, SHARE, 128), BF),
         pltpu.SemaphoreType.DMA((copies,)),
         pltpu.SemaphoreType.DMA((copies,)),
-        pltpu.VMEM((2, 3, 4, HALF, SHARE, c), BF),
-        pltpu.VMEM((2, 3, HALF, SHARE, c), BF),
+        pltpu.VMEM((3, 4, NZH, SHARE, c), BF),
+        pltpu.VMEM((3, NZH, SHARE, c), BF),
     ]
 
 
@@ -235,7 +249,10 @@
 
     barrier = pltpu.get_barrier_semaphore()
     partners = list(ahead) + [at(core=1 - core)]
-    partners += [at(y=lax.rem(y + i, NY), x=lax.rem(x + j, NX)) for i in range(NY) for j in range(NX) if i or j]
+    partners += [at(y=lax.rem(y + j, NY)) for j in range(1, NY)]
+    for j in range(1, N_SLAB):
+        there = lax.rem(slab + j, N_SLAB)
+        partners.append(at(x=there // NZL, zl=lax.rem(there, NZL)))
     z = zh * NZL + zl
     for j in range(1, NZ):
         there = lax.rem(z + j, NZ)
@@ -253,7 +270,8 @@
     lat_load, sends_load, wm_load, nbr_load, edge_load, ws_load, wa_load, wo_load, gains_load, up_load = loads
 
     count = len(bundle_scratch(1))
-    bundles = [Bundle(bundle_refs[i * count : (i + 1) * count], place) for i in range(2 * LAYERS)]
+    bundles = [Bundle(bundle_refs[i * count : (i + 1) * count], place, Y_FIRST[i // 2])
+               for i in range(2 * LAYERS)]
     ret = (ret0, ret1)
     gain = Gains((gain_sums, gain_land, gain_send, gain_recv), place)
 
@@ -416,23 +434,25 @@
             v = dot(adjacency(OWN + 2 * d, 2), gmg[...], 0, 0)
             back[l, d] = v.astype(BF).reshape(2, BLOCK, W)
 
+        one, two = bundles[2 * l], bundles[2 * l + 1]
+
+        def latent_columns(r, l=l):
+            return xs[l, :, :, r].reshape(ROWS, 256)
+
+        def first_grads(l=l):
+            weight_grad(one, 0, (lambda r: hidden[l, :, r], gu.at[l]))
+            weight_grad(one, 1, (latent_columns, gph.at[l]))
+            one.core_start()
+
+        if l == 0:
+            first_grads()
+            gain.start(0)
         copies = halo(
             lambda d: back.at[l, d], lambda d: ret[l].at[d, pl.ds(0, 2)], behind, LAYERS + l, back_grad
         )
 
-        one, two = bundles[2 * l], bundles[2 * l + 1]
-        if earlier:
-            gain.start(0)
-            for bundle in earlier:
-                bundle.plane_done(0)
-                bundle.plane_start(1)
-
-        def latent_columns(r, l=l):
-            return xs[l, :, :, r].reshape(ROWS, 256)
-
-        weight_grad(one, 0, (lambda r: hidden[l, :, r], gu.at[l]))
-        weight_grad(one, 1, (latent_columns, gph.at[l]))
-        one.core_start()
+        if l > 0:
+            first_grads()
         for b in range(OWN):
             r = block_rows(b)
             v = dot(adj[b], gmg[...], 0, 0)
@@ -447,34 +467,38 @@
         weight_grad(two, 0, (lambda r: merged[l, :, r], gph.at[l]))
         weight_grad(two, 1, (latent_columns, gpm), (lambda r: xh[l, :, r], gpmh))
         two.core_start()
+        one.core_done()
+        one.plane_start(0)
         if earlier:
             for bundle in earlier:
-                bundle.plane_done(1)
-                bundle.z_start()
+                bundle.plane_done(0)
+                bundle.plane_start(1)
             gain.done(0)
             gain.start(1)
+        for b in range(OWN):
+            r = block_rows(b)
+            before = up[r].astype(F32) if l == LAYERS - 1 else gy[r]
+            gy[r] = before + dot(gph[l, r], ws[l], 1, 1)
         for d in range(4):
             ret[l][d, 2] = jnp.zeros((BLOCK, W), BF)
-        one.core_done()
-        one.plane_start(0)
-        for b in range(OWN):
-            r = block_rows(b)
-            before = up[r].astype(F32) if l == LAYERS - 1 else gy[r]
-            gy[r] = before + dot(gph[l, r], ws[l], 1, 1)
         two.core_done()
         two.plane_start(0)
         if earlier:
             gain.done(1)
             gain.start(2)
-            z_to_gather(*earlier)
-            for bundle in (one, two):
-                bundle.plane_done(0)
-                bundle.plane_start(1)
+            one.plane_done(0)
+            one.plane_start(1)
+            for bundle in earlier:
+                bundle.plane_done(1)
+            two.plane_done(0)
+            two.plane_start(1)
             gain.done(2)
             gain.start(3)
-            put_all(l + 1, *earlier)
-            for bundle in (one, two):
-                bundle.plane_done(1)
+            one.plane_done(1)
+            one.z_start()
+            two.plane_done(1)
+            two.z_start()
+            for bundle in earlier:
                 bundle.z_start()
         for d in ORDER:
             copies[d].wait()
@@ -497,10 +521,12 @@
 
     grad_copy = pltpu.make_async_copy(gy, grad_out, out_sem.at[1])
     grad_copy.start()
+    gain.done(3)
     z_to_gather(*earlier)
-    gain.done(3)
+    z_to_gather(*bundles[2 * LAYERS - 2 :])
     put_gains()
     put_all(0, *earlier)
+    put_all(LAYERS - 1, *bundles[2 * LAYERS - 2 :])
     out_copy.wait()
     grad_copy.wait()
 

time: 114 us -> 107 us (0.939)
  Pallas kernels: 113 us -> 106 us
    pallas_call x1, Pallas kernels: 110 us -> 104 us  [local(): pl.pallas_call(kernel, out_shape=shapes, in_specs=[hbm] * 10, out_specs=(...]
where the time goes in v4:
time: 107 us
  Pallas kernels  106 us (99%)
    pallas_call x1, Pallas kernels, local(): pl.pallas_call(kernel, out_shape=shapes, in_specs=[hbm] * 10, out_specs=(...  104 us
    pallas_call x1, Pallas kernels, local(): pl.pallas_call(hand_over, out_shape=shapes, in_specs=[hbm] * 7, out_specs...  2.36 us

profile of v4, /device:TPU:8, one launch (start us, length us, event | category | flops | bytes accessed | tf_op | source)
XLA Modules:
  0.0 107.1 jit_solution(2671437877227868198)
XLA Ops:
  0.6 103.9 %shard_map.153 = (bf16[4,128,512]{2,1,0:T(8,128)(2,1)}, f32[512,512]{1,0:T(8,128)}, f32[2,16,512]{2,1,0:T(8,128)}, f32[2,16,512]{2,1,0:T(8,128)}, f32[2,16,512]{...) custom-call(bf16[4,128,512]{2,1,0:T(8,128)(2,1)} %bitcast.3, bf16[512,512]{1,0:T(8,128)(2,1)} %up_in.1, ...), custom_call_target="tpu_custom_call" | custom-call | flops 10000000000 | bytes 10485760 | tf_op jit(solution)/shard_map/pallas_call | solution.py:617
  104.6 2.4 %shard_map.154 = (bf16[4,128,512]{2,1,0:T(8,128)(2,1)}, f32[512,512]{1,0:T(8,128)}, f32[2,16,512]{2,1,0:T(8,128)}, f32[2,16,512]{2,1,0:T(8,128)}, f32[2,16,512]{...) custom-call(bf16[4,128,512]{2,1,0:T(8,128)(2,1)} %get-tuple-element.21.refs_0_, ...), custom_call_target="tpu_custom_call" | custom-call | tf_op jit(solution)/shard_map/pallas_call | solution.py:628

commit v5 on v4

--- a/solution.py
+++ b/solution.py
@@ -484,12 +484,10 @@
         two.core_done()
         two.plane_start(0)
         if earlier:
+            one.plane_done(0)
+            one.plane_start(1)
             gain.done(1)
             gain.start(2)
-            one.plane_done(0)
-            one.plane_start(1)
-            for bundle in earlier:
-                bundle.plane_done(1)
             two.plane_done(0)
             two.plane_start(1)
             gain.done(2)
@@ -499,6 +497,7 @@
             two.plane_done(1)
             two.z_start()
             for bundle in earlier:
+                bundle.plane_done(1)
                 bundle.z_start()
         for d in ORDER:
             copies[d].wait()

time: 107 us -> 107 us (level)
  no operation moved by 1% of the time
where the time goes in v5:
time: 107 us
  Pallas kernels  106 us (99%)
    pallas_call x1, Pallas kernels, local(): pl.pallas_call(kernel, out_shape=shapes, in_specs=[hbm] * 10, out_specs=(...  104 us
    pallas_call x1, Pallas kernels, local(): pl.pallas_call(hand_over, out_shape=shapes, in_specs=[hbm] * 7, out_specs...  2.36 us

profile of v5, /device:TPU:8, one launch (start us, length us, event | category | flops | bytes accessed | tf_op | source)
XLA Modules:
  0.0 107.1 jit_solution(14744371116205126705)
XLA Ops:
  0.6 104.0 %shard_map.153 = (bf16[4,128,512]{2,1,0:T(8,128)(2,1)}, f32[512,512]{1,0:T(8,128)}, f32[2,16,512]{2,1,0:T(8,128)}, f32[2,16,512]{2,1,0:T(8,128)}, f32[2,16,512]{...) custom-call(bf16[4,128,512]{2,1,0:T(8,128)(2,1)} %bitcast.3, bf16[512,512]{1,0:T(8,128)(2,1)} %up_in.1, ...), custom_call_target="tpu_custom_call" | custom-call | flops 10000000000 | bytes 10485760 | tf_op jit(solution)/shard_map/pallas_call | solution.py:616
  104.6 2.4 %shard_map.154 = (bf16[4,128,512]{2,1,0:T(8,128)(2,1)}, f32[512,512]{1,0:T(8,128)}, f32[2,16,512]{2,1,0:T(8,128)}, f32[2,16,512]{2,1,0:T(8,128)}, f32[2,16,512]{...) custom-call(bf16[4,128,512]{2,1,0:T(8,128)(2,1)} %get-tuple-element.21.refs_0_, ...), custom_call_target="tpu_custom_call" | custom-call | tf_op jit(solution)/shard_map/pallas_call | solution.py:627
